TPU v7x, 32 devices: a whole 2x2x4 slice. The times are simulated.
32 devices in a mesh: head: 4 (over y, x), row: 8 (over z, core).
Axes of the slice: x: 2, y: 2, z: 4, core: 2. Of those that a mesh axis runs over, the one named last changes fastest.
Arguments:
- token_ids: int32 [16384], P('row'), may hold values from 0 to 30719
- segment_ids: int32 [16384], P('row'), may hold values from 0 to 511, as said below
- masked_pos: int32 [8, 256], P('row'), may hold values from 0 to 2047, as said below
- masked_target: int32 [8, 256], P('row'), may hold values from 0 to 30719
- embedding: float32 [30720, 768], P(('head', 'row')), may hold values from -1 to 1
- position_table: float32 [512, 768], P(None, ('head', 'row')), may hold values from -0.3 to 0.3
- qkv_weight: float32 [768, 2304], P('row', 'head'), may hold values from -0.21875 to 0.21875
- out_weight: float32 [768, 768], P(None, ('head', 'row')), may hold values from -0.625 to 0.625
- up_weight: float32 [768, 3072], P(None, ('head', 'row')), may hold values from -0.21875 to 0.21875
- down_weight: float32 [3072, 768], P(('head', 'row')), may hold values from -0.109375 to 0.109375
- norm_params: float32 [8, 768], P(None, ('head', 'row')), may hold values from -1 to 4
- up_bias: float32 [3072], P(('head', 'row')), may hold values from -2.5 to 2.5
- m_embedding: float32 [30720, 768], P(('head', 'row')), may hold values from -2.3841858e-06 to 2.3841858e-06
- m_position: float32 [512, 768], P(None, ('head', 'row')), may hold values from -2.3841858e-06 to 2.3841858e-06
- m_qkv: float32 [768, 2304], P('row', 'head'), may hold values from -2.3841858e-06 to 2.3841858e-06
- m_out: float32 [768, 768], P(None, ('head', 'row')), may hold values from -2.3841858e-06 to 2.3841858e-06
- m_up: float32 [768, 3072], P(None, ('head', 'row')), may hold values from -2.3841858e-06 to 2.3841858e-06
- m_down: float32 [3072, 768], P(('head', 'row')), may hold values from -2.3841858e-06 to 2.3841858e-06
- m_norm: float32 [8, 768], P(None, ('head', 'row')), may hold values from -9.536743e-06 to 9.536743e-06
- m_bias: float32 [3072], P(('head', 'row')), may hold values from -9.536743e-06 to 9.536743e-06
- v_embedding: float32 [30720, 768], P(('head', 'row')), may hold values from 1.2872796e-14 to 5.1491184e-14
- v_position: float32 [512, 768], P(None, ('head', 'row')), may hold values from 1.2872796e-14 to 5.1491184e-14
- v_qkv: float32 [768, 2304], P('row', 'head'), may hold values from 1.2872796e-14 to 5.1491184e-14
- v_out: float32 [768, 768], P(None, ('head', 'row')), may hold values from 1.2872796e-14 to 5.1491184e-14
- v_up: float32 [768, 3072], P(None, ('head', 'row')), may hold values from 1.2872796e-14 to 5.1491184e-14
- v_down: float32 [3072, 768], P(('head', 'row')), may hold values from 1.2872796e-14 to 5.1491184e-14
- v_norm: float32 [8, 768], P(None, ('head', 'row')), may hold values from 2.0596473e-13 to 8.2385894e-13
- v_bias: float32 [3072], P(('head', 'row')), may hold values from 5.1491184e-14 to 2.0596473e-13
Outputs:
- new_embedding: float32 [30720, 768], P(('head', 'row'))
- new_position: float32 [512, 768], P(None, ('head', 'row'))
- new_qkv: float32 [768, 2304], P('row', 'head')
- new_out: float32 [768, 768], P(None, ('head', 'row'))
- new_up: float32 [768, 3072], P(None, ('head', 'row'))
- new_down: float32 [3072, 768], P(('head', 'row'))
- new_norm: float32 [8, 768], P(None, ('head', 'row'))
- new_bias: float32 [3072], P(('head', 'row'))
- new_m_embedding: float32 [30720, 768], P(('head', 'row'))
- new_m_position: float32 [512, 768], P(None, ('head', 'row'))
- new_m_qkv: float32 [768, 2304], P('row', 'head')
- new_m_out: float32 [768, 768], P(None, ('head', 'row'))
- new_m_up: float32 [768, 3072], P(None, ('head', 'row'))
- new_m_down: float32 [3072, 768], P(('head', 'row'))
- new_m_norm: float32 [8, 768], P(None, ('head', 'row'))
- new_m_bias: float32 [3072], P(('head', 'row'))
- new_v_embedding: float32 [30720, 768], P(('head', 'row'))
- new_v_position: float32 [512, 768], P(None, ('head', 'row'))
- new_v_qkv: float32 [768, 2304], P('row', 'head')
- new_v_out: float32 [768, 768], P(None, ('head', 'row'))
- new_v_up: float32 [768, 3072], P(None, ('head', 'row'))
- new_v_down: float32 [3072, 768], P(('head', 'row'))
- new_v_norm: float32 [8, 768], P(None, ('head', 'row'))
- new_v_bias: float32 [3072], P(('head', 'row'))
- loss_sum: float32 [], replicated
- live_count: float32 [], replicated
- grad_norm: float32 [], replicated
Inputs may be any that keep to these rules, and one draw needn't show every extreme that they name: `segment_ids`: within each sequence of 512 tokens the documents are numbered from 0 upward, never falling; the tokens after the last document carry 512 - 1 and form padding, which every sequence has. `masked_pos`: entry k of a row lies in [8 k, 8 k + 8) among the group's 2048 tokens.
All inputs are finite; a program needn't handle non-finite values.
Results may differ from a plain program's by a relative error of at most 0.019.
The roundings to bfloat16 on the way count: a program that leaves them out, or rounds other values in their place, can miss the bound.
Values may be sent and summed in bfloat16 or wider, within the bound.
A program may use at most 256 MiB of HBM per device.

v0:
```python
import jax
import jax.numpy as jnp
from jax import lax
from jax.sharding import PartitionSpec as P

HD = 64
SEQ = 512
STEP = 5
RAMP = 10
OLD_HEADS = 8
OLD_FF = 2048


EPSILON = 1e-05
LEARN_RATE = 0.03
GAIN_RATE = 0.5
BETA_ONE = 0.9
BETA_TWO = 0.999
ADAM_EPSILON = 1e-08
DECAY = 0.01
CLIP = 0.02


def combined_all(value, axis, join):
    pieces = jax.tree.map(lambda part: lax.all_gather(part, axis), value)
    head = jax.tree.map(lambda part: part[0], pieces)
    tail = jax.tree.map(lambda part: part[1:], pieces)
    so_far, _ = lax.scan(lambda so_far, piece: (join(so_far, piece), None), head, tail)
    return so_far


def contract(left, right, left_dim, right_dim):
    return lax.dot_general(
        left, right, (((left_dim,), (right_dim,)), ((), ())), preferred_element_type=jnp.float32
    )


def normalize(values, gain, shift):
    center = values - jnp.mean(values, axis=-1, keepdims=True)
    scale = lax.rsqrt(jnp.mean(center * center, axis=-1, keepdims=True) + EPSILON)
    unit = center * scale
    return (unit * gain + shift, unit, scale)


def normalize_back(grad, unit, scale, gain):
    inner = grad * gain
    back = scale * (
        inner
        - jnp.mean(inner, axis=-1, keepdims=True)
        - unit * jnp.mean(inner * unit, axis=-1, keepdims=True)
    )
    return (back, grad * unit)


def score_block(query, keys, labels):
    scores = jnp.einsum("qhe,khe->hqk", query, keys, preferred_element_type=jnp.float32) * HD ** (
        -0.5
    )
    allowed = labels[:, None] == labels[None, :]
    return jnp.where(allowed[None], scores, -1000000000.0)


def attend_fwd(block):
    query, keys, values, labels = block
    scores = score_block(query, keys, labels)
    top = jnp.max(scores, axis=-1, keepdims=True)
    weights = jnp.exp(scores - top)
    total = jnp.sum(weights, axis=-1, keepdims=True)
    probs = weights / total
    output = jnp.einsum(
        "hqk,khe->qhe", probs.astype(jnp.bfloat16), values, preferred_element_type=jnp.float32
    )
    return (output, (top + jnp.log(total))[..., 0])


def attend_back(block):
    query, keys, values, labels, summary, grad_out = block
    scores = score_block(query, keys, labels)
    probs = jnp.exp(scores - summary[..., None])
    grad_values = jnp.einsum(
        "hqk,qhe->khe", probs.astype(jnp.bfloat16), grad_out, preferred_element_type=jnp.float32
    )
    grad_probs = jnp.einsum("qhe,khe->hqk", grad_out, values, preferred_element_type=jnp.float32)
    grad_scores = probs * (grad_probs - jnp.sum(grad_probs * probs, axis=-1, keepdims=True))
    grad_low = grad_scores.astype(jnp.bfloat16)
    grad_query = jnp.einsum(
        "hqk,khe->qhe", grad_low, keys, preferred_element_type=jnp.float32
    ) * HD ** (-0.5)
    grad_keys = jnp.einsum(
        "hqk,qhe->khe", grad_low, query, preferred_element_type=jnp.float32
    ) * HD ** (-0.5)
    return jnp.stack([grad_query, grad_keys, grad_values], axis=2)


def combine_stats(left, right):
    top = jnp.maximum(left[0], right[0])
    total = left[1] * jnp.exp(left[0] - top) + right[1] * jnp.exp(right[0] - top)
    return (top, total, left[2] + right[2])


def adamw(weight, grad, first, second, decay, rate):
    first = BETA_ONE * first + (1 - BETA_ONE) * grad
    second = BETA_TWO * second + (1 - BETA_TWO) * grad * grad
    moved = first / (1 - BETA_ONE**STEP) / (jnp.sqrt(second / (1 - BETA_TWO**STEP)) + ADAM_EPSILON)
    return (weight - rate * (moved + decay * weight), first, second)


def on_device(
    token_ids,
    segment_ids,
    masked_pos,
    masked_target,
    embedding,
    position_table,
    qkv_weight,
    out_weight,
    up_weight,
    down_weight,
    norm_params,
    up_bias,
    m_embedding,
    m_position,
    m_qkv,
    m_out,
    m_up,
    m_down,
    m_norm,
    m_bias,
    v_embedding,
    v_position,
    v_qkv,
    v_out,
    v_up,
    v_down,
    v_norm,
    v_bias,
):
    heads_axis = lax.axis_size("head")
    quarter = lax.axis_index("head")
    table, qkv_full = (
        lax.all_gather(embedding.astype(jnp.bfloat16), "row", axis=0, tiled=True),
        lax.all_gather(qkv_weight.astype(jnp.bfloat16), "row", axis=0, tiled=True),
    )
    places, out_full, up_full, down_full, norms_low, bias_low = (
        lax.all_gather(position_table.astype(jnp.bfloat16), ("head", "row"), axis=1, tiled=True),
        lax.all_gather(out_weight.astype(jnp.bfloat16), ("head", "row"), axis=1, tiled=True),
        lax.all_gather(up_weight.astype(jnp.bfloat16), ("head", "row"), axis=1, tiled=True),
        lax.all_gather(down_weight.astype(jnp.bfloat16), ("head", "row"), axis=0, tiled=True),
        lax.all_gather(norm_params.astype(jnp.bfloat16), ("head", "row"), axis=1, tiled=True),
        lax.all_gather(up_bias.astype(jnp.bfloat16), ("head", "row"), axis=0, tiled=True),
    )
    norms = norms_low.astype(jnp.float32)
    tokens = token_ids.shape[0]
    rows = tokens // heads_axis
    width = table.shape[1]
    vocab_part = table.shape[0]
    local_heads = qkv_full.shape[1] // (3 * HD)
    sequences = tokens // SEQ
    offset = quarter * rows
    local_ids = token_ids - quarter * vocab_part
    inside = (local_ids >= 0) & (local_ids < vocab_part)
    clipped = jnp.clip(local_ids, 0, vocab_part - 1)
    picked = jnp.where(inside[:, None], table[clipped].astype(jnp.float32), 0.0)
    looked = lax.psum(picked.astype(jnp.bfloat16), "head").astype(jnp.float32)
    start_sum = (looked.reshape(sequences, SEQ, width) + places.astype(jnp.float32)[None]).reshape(
        tokens, width
    )
    normed, unit_zero, scale_zero = normalize(start_sum, norms[0], norms[1])
    normed_low = normed.astype(jnp.bfloat16)
    mixed = jnp.dot(normed_low, qkv_full, preferred_element_type=jnp.float32).astype(jnp.bfloat16)
    mixed = mixed.reshape(sequences, SEQ, local_heads, 3, HD)
    labels = segment_ids.reshape(sequences, SEQ)
    query, keys, values = (mixed[:, :, :, 0], mixed[:, :, :, 1], mixed[:, :, :, 2])
    attended, summary = lax.map(attend_fwd, (query, keys, values, labels))
    head_ids = quarter * local_heads + jnp.arange(local_heads)
    head_ramp = jnp.where(head_ids < OLD_HEADS, 1.0, STEP / RAMP).astype(jnp.float32)
    heads_low = (
        (attended * head_ramp[:, None]).astype(jnp.bfloat16).reshape(tokens, local_heads * HD)
    )
    gathered_heads = lax.all_to_all(heads_low, "head", split_axis=0, concat_axis=1, tiled=True)
    projected = jnp.dot(gathered_heads, out_full, preferred_element_type=jnp.float32)
    normed_own = lax.dynamic_slice_in_dim(normed, offset, rows, 0)
    hidden, unit_one, scale_one = normalize(normed_own + projected + norms[6], norms[2], norms[3])
    hidden_low = hidden.astype(jnp.bfloat16)
    upper = jnp.dot(hidden_low, up_full, preferred_element_type=jnp.float32) + bias_low.astype(
        jnp.float32
    )
    neuron_ramp = jnp.where(jnp.arange(upper.shape[1]) < OLD_FF, 1.0, STEP / RAMP).astype(
        jnp.float32
    )
    activated, gelu_pull = jax.vjp(
        lambda inner: jax.nn.gelu(inner, approximate=False) * neuron_ramp, upper
    )
    active_low = activated.astype(jnp.bfloat16)
    lowered = jnp.dot(active_low, down_full, preferred_element_type=jnp.float32) + norms[7]
    final, unit_two, scale_two = normalize(hidden + lowered, norms[4], norms[5])
    chosen_all = masked_pos[0]
    slots = chosen_all.shape[0] // heads_axis
    chosen_own = lax.dynamic_slice_in_dim(chosen_all, quarter * slots, slots, 0) - offset
    all_rows = lax.all_gather(final[chosen_own].astype(jnp.bfloat16), "head", axis=0, tiled=True)
    valid = (segment_ids[chosen_all] != SEQ - 1).astype(jnp.float32)
    logits = contract(all_rows, table, 1, 1)
    targets_local = masked_target[0] - quarter * vocab_part
    hits = jnp.arange(vocab_part)[None, :] == targets_local[:, None]
    top = jnp.max(logits, axis=1)
    sums = jnp.sum(jnp.exp(logits - top[:, None]), axis=1)
    target_part = jnp.sum(jnp.where(hits, logits, 0.0), axis=1)
    top_all, sums_all, target_all = combined_all((top, sums, target_part), "head", combine_stats)
    log_total = top_all + jnp.log(sums_all)
    row_loss = (log_total - target_all) * valid
    loss_own = jnp.sum(lax.dynamic_slice_in_dim(row_loss, quarter * slots, slots, 0))
    count_own = jnp.sum(lax.dynamic_slice_in_dim(valid, quarter * slots, slots, 0))
    grad_logits = (
        valid[:, None] * (jnp.exp(logits - log_total[:, None]) - hits.astype(jnp.float32))
    ).astype(jnp.bfloat16)
    grad_table = contract(grad_logits, all_rows, 0, 0)
    grad_picked = lax.psum_scatter(
        jnp.dot(grad_logits, table, preferred_element_type=jnp.float32),
        "head",
        scatter_dimension=0,
        tiled=True,
    )
    grad_final = jnp.zeros((rows, width), jnp.float32).at[chosen_own].add(grad_picked)
    grad_sum, gain_two = normalize_back(grad_final, unit_two, scale_two, norms[4])
    grad_sum_low = grad_sum.astype(jnp.bfloat16)
    grad_down = contract(active_low, grad_sum_low, 0, 0)
    grad_upper = gelu_pull(contract(grad_sum_low, down_full, 1, 1))[0]
    grad_upper_low = grad_upper.astype(jnp.bfloat16)
    grad_up = contract(hidden_low, grad_upper_low, 0, 0)
    grad_hidden = grad_sum + contract(grad_upper_low, up_full, 1, 1)
    grad_res, gain_one = normalize_back(grad_hidden, unit_one, scale_one, norms[2])
    grad_res_low = grad_res.astype(jnp.bfloat16)
    grad_out = contract(gathered_heads, grad_res_low, 0, 0)
    grad_heads = lax.all_to_all(
        contract(grad_res_low, out_full, 1, 1).astype(jnp.bfloat16),
        "head",
        split_axis=1,
        concat_axis=0,
        tiled=True,
    )
    grad_attended = (
        grad_heads.reshape(sequences, SEQ, local_heads, HD).astype(jnp.float32) * head_ramp[:, None]
    ).astype(jnp.bfloat16)
    grad_mixed = lax.map(attend_back, (query, keys, values, labels, summary, grad_attended))
    grad_mixed_low = grad_mixed.reshape(tokens, local_heads * 3 * HD).astype(jnp.bfloat16)
    grad_qkv = contract(normed_low, grad_mixed_low, 0, 0)
    grad_input = contract(grad_mixed_low, qkv_full, 1, 1)
    grad_input = lax.dynamic_update_slice_in_dim(
        grad_input, lax.dynamic_slice_in_dim(grad_input, offset, rows, 0) + grad_res, offset, 0
    )
    grad_normed = lax.psum(grad_input.astype(jnp.bfloat16), "head").astype(jnp.float32)
    grad_start, gain_zero = normalize_back(grad_normed, unit_zero, scale_zero, norms[0])
    grad_own_start = lax.dynamic_slice_in_dim(grad_start, offset, rows, 0)
    grad_places = jnp.sum(grad_own_start.reshape(rows // SEQ, SEQ, width), axis=0)
    grad_table = grad_table.at[clipped].add(jnp.where(inside[:, None], grad_start, 0.0))
    grad_norms = jnp.stack(
        [
            jnp.sum(lax.dynamic_slice_in_dim(gain_zero, offset, rows, 0), axis=0),
            jnp.sum(lax.dynamic_slice_in_dim(grad_normed, offset, rows, 0), axis=0),
            jnp.sum(gain_one, axis=0),
            jnp.sum(grad_hidden, axis=0),
            jnp.sum(gain_two, axis=0),
            jnp.sum(grad_final, axis=0),
            jnp.sum(grad_res, axis=0),
            jnp.sum(grad_sum, axis=0),
        ]
    )
    grad_bias = jnp.sum(grad_upper, axis=0)
    grad_table, grad_qkv = (
        lax.psum_scatter(grad_table, "row", scatter_dimension=0, tiled=True),
        lax.psum_scatter(grad_qkv, "row", scatter_dimension=0, tiled=True),
    )
    grad_places, grad_out, grad_up, grad_down, grad_norms, grad_bias = (
        lax.psum_scatter(grad_places, ("head", "row"), scatter_dimension=1, tiled=True),
        lax.psum_scatter(grad_out, ("head", "row"), scatter_dimension=1, tiled=True),
        lax.psum_scatter(grad_up, ("head", "row"), scatter_dimension=1, tiled=True),
        lax.psum_scatter(grad_down, ("head", "row"), scatter_dimension=0, tiled=True),
        lax.psum_scatter(grad_norms, ("head", "row"), scatter_dimension=1, tiled=True),
        lax.psum_scatter(grad_bias, ("head", "row"), scatter_dimension=0, tiled=True),
    )
    grads = (grad_table, grad_places, grad_qkv, grad_out, grad_up, grad_down, grad_norms, grad_bias)
    squares = sum((jnp.sum(g * g) for g in grads))
    squares, loss_sum, live_count = lax.psum((squares, loss_own, count_own), ("head", "row"))
    grad_norm = jnp.sqrt(squares) / live_count
    factor = jnp.minimum(1.0, CLIP / grad_norm) / live_count
    params = (
        embedding,
        position_table,
        qkv_weight,
        out_weight,
        up_weight,
        down_weight,
        norm_params,
        up_bias,
    )
    firsts = (m_embedding, m_position, m_qkv, m_out, m_up, m_down, m_norm, m_bias)
    seconds = (v_embedding, v_position, v_qkv, v_out, v_up, v_down, v_norm, v_bias)
    decays = (DECAY, DECAY, DECAY, DECAY, DECAY, DECAY, 0.0, 0.0)
    rates = (
        LEARN_RATE,
        LEARN_RATE,
        LEARN_RATE,
        LEARN_RATE,
        LEARN_RATE,
        LEARN_RATE,
        GAIN_RATE,
        GAIN_RATE,
    )
    results = [
        adamw(w, g * factor, m, v, d, r)
        for w, g, m, v, d, r in zip(params, grads, firsts, seconds, decays, rates)
    ]
    news = [r[0] for r in results]
    moms = [r[1] for r in results]
    secs = [r[2] for r in results]
    return (
        news[0],
        news[1],
        news[2],
        news[3],
        news[4],
        news[5],
        news[6],
        news[7],
        moms[0],
        moms[1],
        moms[2],
        moms[3],
        moms[4],
        moms[5],
        moms[6],
        moms[7],
        secs[0],
        secs[1],
        secs[2],
        secs[3],
        secs[4],
        secs[5],
        secs[6],
        secs[7],
        loss_sum,
        live_count,
        grad_norm,
    )


def solution(mesh):
    placed = (
        P("row"),
        P("row"),
        P("row", None),
        P("row", None),
        P(("head", "row"), None),
        P(None, ("head", "row")),
        P("row", "head"),
        P(None, ("head", "row")),
        P(None, ("head", "row")),
        P(("head", "row"), None),
        P(None, ("head", "row")),
        P(("head", "row")),
        P(("head", "row"), None),
        P(None, ("head", "row")),
        P("row", "head"),
        P(None, ("head", "row")),
        P(None, ("head", "row")),
        P(("head", "row"), None),
        P(None, ("head", "row")),
        P(("head", "row")),
        P(("head", "row"), None),
        P(None, ("head", "row")),
        P("row", "head"),
        P(None, ("head", "row")),
        P(None, ("head", "row")),
        P(("head", "row"), None),
        P(None, ("head", "row")),
        P(("head", "row")),
    )
    return jax.shard_map(
        on_device,
        mesh=mesh,
        in_specs=placed,
        out_specs=(
            P(("head", "row"), None),
            P(None, ("head", "row")),
            P("row", "head"),
            P(None, ("head", "row")),
            P(None, ("head", "row")),
            P(("head", "row"), None),
            P(None, ("head", "row")),
            P(("head", "row")),
            P(("head", "row"), None),
            P(None, ("head", "row")),
            P("row", "head"),
            P(None, ("head", "row")),
            P(None, ("head", "row")),
            P(("head", "row"), None),
            P(None, ("head", "row")),
            P(("head", "row")),
            P(("head", "row"), None),
            P(None, ("head", "row")),
            P("row", "head"),
            P(None, ("head", "row")),
            P(None, ("head", "row")),
            P(("head", "row"), None),
            P(None, ("head", "row")),
            P(("head", "row")),
            P(),
            P(),
            P(),
        ),
        check_vma=False,
    )
```

profile of v0, /device:TPU:0, one launch (start us, length us, event | category | flops | bytes accessed | tf_op | source)
XLA Modules:
  0.0 1373.8 jit_solution(16962763606275622722)
XLA Ops:
  11.9 112.4 %all-gather.12.cloned.1.call-done = bf16[7680,768]{1,0:T(8,128)(2,1)} async-done(((bf16[960,768]{1,0:T(8,128)(2,1)}), bf16[7680,768]{1,0:T(8,128)(2,1)}) %all-gather.12.cloned.1.call-update) | async-done | bytes 11796496 | tf_op jit(solution)/shard_map/all_gather | solution.py:141
  124.3 14.3 %gather_fusion.1 = bf16[2048,768]{1,0:T(8,128)(2,1)S(1)} fusion(bf16[7680,768]{1,0:T(8,128)(2,1)} %all-gather.12.cloned.1.call-done, s32[2048]{0:T(1024)S(1)} %get-tuple-element.338), kind=kCustom, calls=%fused_computation.1 | custom fusion | bytes 6299648 | tf_op jit(solution)/shard_map/gather | solution.py:163
  143.8 43.0 %all_gather.46 = bf16[512,768]{0,1:T(8,128)(2,1)S(1)} all-gather(bf16[512,24]{0,1:T(8,128)(2,1)S(1)} %convert_element_type.123), channel_id=1, replica_groups=mesh['head'=4,'row'=8] {'head','row'}, dimensions={1}, use_global_device_ids=true | all-gather | bytes 811008 | tf_op jit(solution)/shard_map/all_gather | solution.py:145
  187.1 37.5 %all-gather.3 = bf16[32,24,8]{1,2,0:T(8,128)(2,1)S(1)} all-gather(bf16[1,24,8]{1,2,0:T(8,128)(2,1)S(1)} %convert_bitcast_fusion), channel_id=1, replica_groups=mesh['head'=4,'row'=8] {'head','row'}, dimensions={0}, use_global_device_ids=true | all-gather | bytes 12672 | tf_op jit(solution)/shard_map/all_gather | solution.py:149
  225.1 17.7 %all_gather.48 = bf16[768,576]{1,0:T(8,128)(2,1)S(1)} all-gather(bf16[96,576]{1,0:T(8,128)(2,1)S(1)} %convert_element_type.128), channel_id=1, replica_groups=mesh['head'=4,'row'=8] {'row'}, dimensions={0}, use_global_device_ids=true | all-gather | bytes 995328 | tf_op jit(solution)/shard_map/all_gather | solution.py:142
  264.0 16.6 %while.36 = (s32[]{:T(128)}, f32[4,512,3,64]{1,3,2,0:T(8,128)}, f32[4,3,512]{2,1,0:T(4,128)}, bf16[4,512,3,64]{1,3,2,0:T(8,128)(2,1)S(1)}, s32[4,512]{1,0:T(4,12...) while((s32[]{:T(128)}, f32[4,512,3,64]{1,3,2,0:T(8,128)}, ...), condition=%wide.region_6.7_spmd, body=%wide.region_3.6_spmd.sunk | while | flops 211024384 | bytes 11532889 | solution.py:174
  287.9 46.0 %all-reduce = bf16[3072]{0:T(1024)(128)(2,1)S(1)} all-reduce(bf16[3072]{0:T(1024)(128)(2,1)S(1)} %dynamic-update-slice), channel_id=1, replica_groups=mesh['head'=4,'row'=8] {'head','row'}, use_global_device_ids=true, to_apply=%add | all-reduce | flops 3072 | bytes 12288
  341.0 20.1 %multiply_convert_fusion.2 = (bf16[512,3072]{1,0:T(8,128)(2,1)}, f32[512,3072]{1,0:T(8,128)}, f32[512,3072]{1,0:T(8,128)}) fusion(f32[3072]{0:T(1024)S(1)} %fusion.83, f32[3072]{0:T(1024)S(1)} %convert_element_type.135, bf16[768,3072]{0,1:T(8,128)(2,1)} %all-gather.16.cloned.1.call-done, f32[512,768]{1,0:T(8,128)S(1)} %get-tuple-element.352, ...), kind=kOutput, calls=%fused_computation.78 | convolution fusion | flops 2523267072 | bytes 22054912 | tf_op jit(solution)/shard_map/dot_general | solution.py:185
  369.2 11.3 all_gather.53
  412.9 11.8 fusion.93
  424.8 24.5 %reduce-scatter.11.cloned.1.call-done = f32[64,768]{1,0:T(8,128)} async-done(((f32[256,768]{1,0:T(8,128)}), f32[64,768]{1,0:T(8,128)}) %reduce-scatter.11.cloned.1.call-update) | async-done | bytes 196624 | tf_op jit(solution)/shard_map/reduce_scatter | solution.py:217
  455.3 10.0 fusion.110
  476.8 10.9 all-to-all-done.1
  490.2 27.1 %while.38 = (s32[]{:T(128)}, bf16[4,512,3,3,64]{1,4,2,3,0:T(8,128)(2,1)}, bf16[4,512,3,64]{1,3,2,0:T(8,128)(2,1)S(1)}, s32[4,512]{1,0:T(4,128)S(1)}, bf16[4,512,...) while((s32[]{:T(128)}, ...), condition=%wide.region_24.25_spmd, body=%wide.region_22.24_spmd.sunk | while | flops 512817664 | bytes 30450316 | solution.py:244
  530.8 8.6 fusion.63
  539.5 75.3 %all-reduce.10.cloned.1.call-done = bf16[2048,768]{1,0:T(8,128)(2,1)} async-done(((bf16[2048,768]{1,0:T(8,128)(2,1)}), bf16[2048,768]{1,0:T(8,128)(2,1)}) %all-reduce.10.cloned.1.call-update) | async-done | bytes 3145744 | tf_op jit(solution)/shard_map/psum | solution.py:251
  645.0 16.2 %fusion.94 = f32[7680,768]{1,0:T(8,128)} fusion(bf16[256,768]{1,0:T(8,128)(2,1)S(1)} %all_gather.53, f32[256,7680]{1,0:T(8,128)} %copy-done.3, f32[256]{0:T(256)S(1)} %copy-done.75, s32[256]{0:T(256)S(1)} %bitcast.241, f32[256]{0:T(256)S(1)} %copy-done.73), kind=kOutput, calls=%fused_computation.233 | convolution fusion | flops 3031695360 | bytes 31853568 | tf_op jit(solution)/shard_map/dot_general | solution.py:33
  661.1 31.5 %scatter_custom_fusion.1 = f32[7680,768]{1,0:T(8,128)} fusion(f32[7680,768]{1,0:T(8,128)} %fusion.94, s32[2048]{0:T(1024)} %get-tuple-element.339, f32[2048,768]{1,0:T(8,128)} %copy-done.6, f32[]{:T(128)} %constant.94.clone.1, pred[2048]{0:T(1024)(128)(4,1)S(1)} %copy-done.55), kind=kCustom, calls=%fused_computation.73 | custom fusion | flops 3145728 | bytes 29886976 | tf_op jit(solution)/shard_map/scatter-add | solution.py:255
  698.1 40.0 %all-reduce.4 = (f32[8,768]{1,0:T(8,128)S(1)}, f32[3072]{0:T(1024)S(1)}) all-reduce(f32[8,768]{1,0:T(8,128)S(1)} %stack.47, f32[3072]{0:T(1024)S(1)} %copy-done.71), channel_id=12, replica_groups=mesh['head'=4,'row'=8] {'head','row'}, use_global_device_ids=true, to_apply=%region_51.52.clone | all-reduce | flops 9216 | bytes 73728
  741.1 40.9 %reduce-scatter.23.cloned.1.call-done = f32[24,512]{1,0:T(8,128)} async-done(((f32[768,512]{1,0:T(8,128)}), f32[24,512]{1,0:T(8,128)}) %reduce-scatter.23.cloned.1.call-update) | async-done | bytes 49168
  783.6 138.9 %reduce-scatter.19.cloned.1.call-done = f32[768,96]{0,1:T(8,128)} async-done(((f32[768,3072]{0,1:T(8,128)}), f32[768,96]{0,1:T(8,128)}) %reduce-scatter.19.cloned.1.call-update) | async-done | bytes 294928 | tf_op jit(solution)/shard_map/reduce_scatter | solution.py:276
  924.1 139.7 %reduce-scatter.21.cloned.1.call-done = f32[96,768]{1,0:T(8,128)} async-done(((f32[3072,768]{1,0:T(8,128)}), f32[96,768]{1,0:T(8,128)}) %reduce-scatter.21.cloned.1.call-update) | async-done | bytes 294928 | tf_op jit(solution)/shard_map/reduce_scatter | solution.py:277
  1065.4 231.7 %reduce-scatter.13.cloned.1.call-done = f32[960,768]{1,0:T(8,128)} async-done(((f32[7680,768]{1,0:T(8,128)}), f32[960,768]{1,0:T(8,128)}) %reduce-scatter.13.cloned.1.call-update) | async-done | bytes 2949136 | tf_op jit(solution)/shard_map/reduce_scatter | solution.py:270
  1305.7 38.3 %all-reduce.3 = (f32[]{:T(128)}, f32[]{:T(128)}, f32[]{:T(128)}) all-reduce(f32[]{:T(128)} %dynamic-slice_reduce_fusion.2, f32[]{:T(128)S(6)} %add.408, f32[]{:T(128)} %dynamic-slice_reduce_fusion.1), channel_id=1, replica_groups=mesh['head'=4,'row'=8] {'head','row'}, use_global_device_ids=true, to_apply=%region_31.32 | all-reduce | flops 3 | bytes 24 | tf_op jit(solution)/shard_map/psum | solution.py:283
  (446 shorter events, 226.9 us)
Async XLA Ops:
  8.0 116.3 %all-gather.12.cloned.1.call-start = ((), (), s32[]{:S(2)}) async-start(), calls=%async_computation.9 | async-start | bytes 13271040 | tf_op jit(solution)/shard_map/all_gather | solution.py:141
  11.2 232.4 %all-reduce.8.cloned.1.call-start = ((), (), s32[]{:S(2)}) async-start(), calls=%async_computation.10 | async-start | bytes 6291456 | tf_op jit(solution)/shard_map/psum | solution.py:164
  11.3 127.4 %copy-start.54 = (pred[2048]{0:T(1024)(128)(4,1)}, pred[2048]{0:T(1024)(128)(4,1)S(1)}, u32[]{:S(2)}) copy-start(pred[2048]{0:T(1024)(128)(4,1)S(1)} %compare_and_fusion) | copy-start | bytes 6148
  140.7 196.1 %all-gather.14.cloned.1.call-start = ((), (), s32[]{:S(2)}) async-start(), calls=%async_computation.11 | async-start | bytes 1216512 | tf_op jit(solution)/shard_map/all_gather | solution.py:146
  142.2 198.8 %all-gather.16.cloned.1.call-start = ((), (), s32[]{:S(2)}) async-start(), calls=%async_computation.12 | async-start | bytes 4866048 | tf_op jit(solution)/shard_map/all_gather | solution.py:147
  143.0 218.2 %all-gather.18.cloned.1.call-start = ((), (), s32[]{:S(2)}) async-start(), calls=%async_computation.13 | async-start | bytes 4866048 | tf_op jit(solution)/shard_map/all_gather | solution.py:148
  225.0 136.1 %copy-start.58 = (f32[768]{0:T(1024)}, f32[768]{0:T(1024)S(1)}, u32[]{:S(2)}) copy-start(f32[768]{0:T(1024)S(1)} %get-tuple-element.251) | copy-start | bytes 9220
  225.1 136.1 %copy-start.81 = (f32[768]{0:T(1024)}, f32[768]{0:T(1024)S(1)}, u32[]{:S(2)}) copy-start(f32[768]{0:T(1024)S(1)} %get-tuple-element.250) | copy-start | bytes 9220
  284.0 52.8 %all-to-all-start = ((bf16[4,512,192]{1,2,0:T(8,128)(2,1)}), bf16[4,512,192]{1,2,0:T(8,128)(2,1)S(1)}, u32[]{:S(2)}, u32[]{:S(2)}) async-start(bf16[4,512,192]{1,2,0:T(8,128)(2,1)} %bitcast.222), calls=%async_computation | async-start | bytes 1572864 | tf_op jit(solution)/shard_map/all_to_all | solution.py:180
  287.5 161.8 %reduce-scatter.11.cloned.1.call-start = ((), (), s32[]{:S(2)}) async-start(), calls=%async_computation.14 | async-start | bytes 983040 | tf_op jit(solution)/shard_map/reduce_scatter | solution.py:217
  472.2 15.5 %all-to-all-start.1 = ((bf16[512,4,192]{0,2,1:T(8,128)(2,1)}), bf16[512,4,192]{0,2,1:T(8,128)(2,1)}, u32[]{:S(2)}, u32[]{:S(2)}) async-start(bf16[512,4,192]{0,2,1:T(8,128)(2,1)} %bitcast.223), calls=%async_computation.2 | async-start | bytes 1572864 | tf_op jit(solution)/shard_map/all_to_all | solution.py:234
  476.6 138.2 %all-reduce.10.cloned.1.call-start = ((), (), s32[]{:S(2)}) async-start(), calls=%async_computation.15 | async-start | bytes 6291456 | tf_op jit(solution)/shard_map/psum | solution.py:251
  527.0 167.3 %reduce-scatter.17.cloned.1.call-start = ((), (), s32[]{:S(2)}) async-start(), calls=%async_computation.18 | async-start | bytes 2433024 | tf_op jit(solution)/shard_map/reduce_scatter | solution.py:275
  530.4 209.1 %reduce-scatter.15.cloned.1.call-start = ((), (), s32[]{:S(2)}) async-start(), calls=%async_computation.17 | async-start | bytes 2211840 | tf_op jit(solution)/shard_map/reduce_scatter | solution.py:271
  539.5 242.6 %reduce-scatter.23.cloned.1.call-start = ((), (), s32[]{:S(2)}) async-start(), calls=%async_computation.21 | async-start | bytes 1622016
  626.4 296.1 %reduce-scatter.19.cloned.1.call-start = ((), (), s32[]{:S(2)}) async-start(), calls=%async_computation.19 | async-start | bytes 9732096 | tf_op jit(solution)/shard_map/reduce_scatter | solution.py:276
  634.8 429.0 %reduce-scatter.21.cloned.1.call-start = ((), (), s32[]{:S(2)}) async-start(), calls=%async_computation.20 | async-start | bytes 9732096 | tf_op jit(solution)/shard_map/reduce_scatter | solution.py:277
  644.3 652.8 %reduce-scatter.13.cloned.1.call-start = ((), (), s32[]{:S(2)}) async-start(), calls=%async_computation.16 | async-start | bytes 26542080 | tf_op jit(solution)/shard_map/reduce_scatter | solution.py:270
  696.3 650.5 %copy-start.95 = (f32[96]{0:T(128)S(1)}, f32[96]{0:T(128)}, u32[]{:S(2)}) copy-start(f32[96]{0:T(128)} %param.45) | copy-start | bytes 1156
  696.3 652.0 %copy-start.66 = (f32[8,24]{1,0:T(8,128)S(1)}, f32[8,24]{1,0:T(8,128)}, u32[]{:S(2)}) copy-start(f32[8,24]{1,0:T(8,128)} %param.44) | copy-start | bytes 2308
  696.3 652.0 %copy-start.85 = (f32[8,24]{1,0:T(8,128)S(1)}, f32[8,24]{1,0:T(8,128)}, u32[]{:S(2)}) copy-start(f32[8,24]{1,0:T(8,128)} %param.52) | copy-start | bytes 2308
  696.3 651.9 %copy-start.86 = (f32[8,24]{1,0:T(8,128)S(1)}, f32[8,24]{1,0:T(8,128)}, u32[]{:S(2)}) copy-start(f32[8,24]{1,0:T(8,128)} %param.60) | copy-start | bytes 2308
  696.3 653.4 %copy-start.28 = (f32[96,768]{1,0:T(8,128)S(1)}, f32[96,768]{1,0:T(8,128)}, u32[]{:S(2)}) copy-start(f32[96,768]{1,0:T(8,128)} %param.43) | copy-start | bytes 884740
  741.1 611.0 %copy-start.30 = (f32[768,96]{0,1:T(8,128)S(1)}, f32[768,96]{0,1:T(8,128)}, u32[]{:S(2)}) copy-start(f32[768,96]{0,1:T(8,128)} %param.42) | copy-start | bytes 884740
  (95 other events, 1504.5 us)
Sparse Core Ops, SparseCore 0:
  11.3 112.9 all-gather.11
  140.8 89.1 all-reduce.7
  424.9 24.3 reduce-scatter.10
  527.1 87.6 all-reduce.9
Sparse Core Ops, SparseCore 1:
  144.8 69.6 all-gather.13
  217.9 64.6 all-gather.15
  286.1 64.9 all-gather.17
  534.5 108.4 reduce-scatter.16
  645.9 34.4 reduce-scatter.14
  686.2 95.7 reduce-scatter.22
  787.8 134.7 reduce-scatter.18
  929.3 134.5 reduce-scatter.20
  1066.0 231.1 reduce-scatter.12
where the time goes:
time: 1380 us; the launch traced here: 1370 us
  waiting for transfers between devices  775 us (56%)
  blocking collectives  256 us (19%)
  matrix products  138 us (10%)
  other arithmetic  122 us (9%)
  local copies, waits for them, and re-layouts  47.9 us (3%)
  between operations  26.3 us (2%)
    reduce_scatter x1, waiting for transfers between devices, on_device(): lax.psum_scatter(grad_table, 'row', scatter_dimension=0, tiled=True)  232 us
    reduce_scatter x1, waiting for transfers between devices, on_device(): lax.psum_scatter(grad_down, ('head', 'row'), scatter_dimension=0, tiled=T...  140 us
    reduce_scatter x1, waiting for transfers between devices, on_device(): lax.psum_scatter(grad_up, ('head', 'row'), scatter_dimension=1, tiled=True)  139 us
    all_gather x1, waiting for transfers between devices, on_device(): lax.all_gather(embedding.astype(jnp.bfloat16), 'row', axis=0, tiled=True)  112 us
    unnamed x2, blocking collectives  85.9 us
    psum x1, waiting for transfers between devices, on_device(): lax.psum(grad_input.astype(jnp.bfloat16), 'head').astype(jnp.float32)  75.3 us
    dot_general x10, matrix products, contract(): lax.dot_general(left, right, (((left_dim,), (right_dim,)), ((), ())), pre...  66.8 us
    all_gather x1, blocking collectives, on_device(): lax.all_gather(position_table.astype(jnp.bfloat16), ('head', 'row'), axis...  43 us
  transfers between devices with their start and end apart: 15, of which 8 were waited for; matrix products, arithmetic and copies ran while one was open for 12% of the time, Pallas kernels for 0%

commit v1 on v0

v1 whole, which is shorter than its diff:
```python
import functools

import jax
import jax.numpy as jnp
from jax import lax
from jax.experimental import pallas as pl
from jax.experimental.pallas import tpu as pltpu
from jax.sharding import PartitionSpec as P

HD = 64
SEQ = 512
STEP = 5
RAMP = 10
OLD_HEADS = 8
OLD_FF = 2048


EPSILON = 1e-05
LEARN_RATE = 0.03
GAIN_RATE = 0.5
BETA_ONE = 0.9
BETA_TWO = 0.999
ADAM_EPSILON = 1e-08
DECAY = 0.01
CLIP = 0.02

ROOM = 64
HEADS = 4
MESH = pl.DeviceIdType.MESH
ANY = pl.BlockSpec(memory_space=pl.ANY)
VMEM = pl.BlockSpec(memory_space=pltpu.VMEM)


def place():
    h = lax.axis_index("head")
    r = lax.axis_index("row")
    return h, lax.div(r, 2), lax.rem(r, 2)


def across(h, q):
    if q == 0:
        return h
    if q == 1:
        return h + 1 - 2 * lax.rem(h, 2)
    if q == 2:
        return lax.rem(h + 2, 4)
    return 3 - h


class Wires:
    def __init__(self, send, recv):
        self.send, self.recv, self.used, self.made = send, recv, 0, []

    def copy(self, src, dst, to):
        i = self.used
        self.used += 1
        one = pltpu.make_async_remote_copy(
            src_ref=src,
            dst_ref=dst,
            send_sem=self.send.at[i],
            recv_sem=self.recv.at[i],
            device_id=to,
            device_id_type=MESH,
        )
        one.start()
        self.made.append(one)
        return one

    def sent(self):
        for one in self.made:
            one.wait_send()


def greet(peers):
    barrier = pltpu.get_barrier_semaphore()
    for to in peers:
        pl.semaphore_signal(barrier, inc=1, device_id=to, device_id_type=MESH)
    pl.semaphore_wait(barrier, len(peers))


def near(planes):
    h, z, c = place()
    peers = [(h, 2 * z + 1 - c), (across(h, 1), 2 * z + c), (across(h, 2), 2 * z + c)]
    peers += [(h, 2 * lax.rem(z + s, planes) + c) for s in range(1, planes)]
    return peers


def every_chip(planes):
    h, z, c = place()
    peers = [(h, 2 * z + 1 - c)]
    for q in range(4):
        for s in range(planes):
            if q or s:
                peers.append((across(h, q), 2 * lax.rem(z + s, planes) + c))
    return peers


def split(rows):
    first = -(-rows // 32) * 16
    return pl.ds(0, first), pl.ds(first, rows - first)


def gather_steps(wires, local, planes, pairs):
    h, z, c = place()
    row = 2 * z + c
    sib = (h, 2 * z + 1 - c)
    hx, hy, hd = across(h, 1), across(h, 2), across(h, 3)
    xn, yn = (hx, row), (hy, row)
    zs = [lax.rem(z - s + planes, planes) for s in range(planes)]
    count = len(pairs)
    here = []
    for k, (x, out) in enumerate(pairs):
        one = pltpu.make_async_copy(x, out.at[h, z, c], local.at[k])
        one.start()
        here.append(one)
    from_z = {}
    for k, (x, out) in enumerate(pairs):
        for s in range(1, planes):
            from_z[k, s] = wires.copy(x, out.at[h, z, c], (h, 2 * lax.rem(z + s, planes) + c))
    from_x, from_y, from_xd, from_yd, from_sib = {}, {}, {}, {}, []

    def launch(k, s):
        x, out = pairs[k]
        src = x if s == 0 else out.at[h, zs[s], c]
        if s:
            from_z[k, s].wait_recv()
        dst = out.at[h, zs[s], c]
        from_x[k, s] = wires.copy(src, dst, xn)
        from_y[k, s] = wires.copy(src, dst, yn)
        from_sib.append(wires.copy(src, dst, sib))

    def relay(k, s):
        _, out = pairs[k]
        first, second = split(out.shape[3])
        from_x[k, s].wait_recv()
        got = out.at[hx, zs[s], c]
        from_yd[k, s] = wires.copy(got.at[second], got.at[second], yn)
        from_sib.append(wires.copy(got, got, sib))
        from_y[k, s].wait_recv()
        got = out.at[hy, zs[s], c]
        from_xd[k, s] = wires.copy(got.at[first], got.at[first], xn)
        from_sib.append(wires.copy(got, got, sib))

    def finish(k, s):
        _, out = pairs[k]
        from_yd[k, s].wait_recv()
        from_xd[k, s].wait_recv()
        got = out.at[hd, zs[s], c]
        from_sib.append(wires.copy(got, got, sib))

    order = [(k, s) for k in range(count) for s in range(planes)]
    for i in range(len(order) + 2):
        if i < len(order):
            launch(*order[i])
        if 1 <= i <= len(order):
            relay(*order[i - 1])
        if i >= 2:
            finish(*order[i - 2])
    for one in from_sib:
        one.wait_recv()
    for one in here:
        one.wait()


def spread_start(wires, local, planes, parcels, out):
    h, z, c = place()
    sib = (h, 2 * z + 1 - c)
    got = {}
    for q in range(4):
        for s in range(planes):
            if q or s:
                th, tz = across(h, q), lax.rem(z + s, planes)
                got[q, s] = wires.copy(parcels(th, tz), out.at[c, h, z], (th, 2 * tz + c))
    mine = pltpu.make_async_copy(parcels(h, z), out.at[c, h, z], local)
    mine.start()
    passed = [wires.copy(parcels(h, z), out.at[c, h, z], sib)]
    return got, mine, passed


def spread_finish(wires, planes, out, state):
    h, z, c = place()
    sib = (h, 2 * z + 1 - c)
    got, mine, passed = state
    for (q, s), one in got.items():
        one.wait_recv()
        there = out.at[c, across(h, q), lax.rem(z - s + planes, planes)]
        passed.append(wires.copy(there, there, sib))
    for one in passed:
        one.wait_recv()
    mine.wait()


def small_kernel(planes, x, out, send, recv, local):
    greet(every_chip(planes))
    wires = Wires(send, recv)
    state = spread_start(wires, local, planes, lambda h, z: x, out)
    spread_finish(wires, planes, out, state)
    wires.sent()


def ids_kernel(planes, x, out, send, recv, local):
    h, z, c = place()
    offsets = [(s, e) for s in range(planes) for e in range(2) if s or e]
    peers = [(h, 2 * lax.rem(z + s, planes) + lax.rem(c + e, 2)) for s, e in offsets]
    greet(peers)
    wires = Wires(send, recv)
    mine = pltpu.make_async_copy(x, out.at[2 * z + c], local)
    mine.start()
    for to in peers:
        wires.copy(x, out.at[2 * z + c], to)
    for one in wires.made:
        one.wait_recv()
    mine.wait()
    wires.sent()


def gather_kernel(planes, count, *refs):
    xs, outs = refs[:count], refs[count : 2 * count]
    send, recv, local = refs[2 * count :]
    greet(near(planes))
    wires = Wires(send, recv)
    gather_steps(wires, local, planes, list(zip(xs, outs)))
    wires.sent()


def fetch_kernel(planes, count, *refs):
    parcels, xs = refs[0], refs[1 : 1 + count]
    out, outs = refs[1 + count], refs[2 + count : 2 + 2 * count]
    send, recv, local = refs[2 + 2 * count :]
    greet(every_chip(planes))
    wires = Wires(send, recv)
    state = spread_start(wires, local.at[count], planes, lambda h, z: parcels.at[h, z], out)
    gather_steps(wires, local, planes, list(zip(xs, outs)))
    spread_finish(wires, planes, out, state)
    wires.sent()


def deliver_kernel(planes, parcels, out, send, recv, local):
    greet(every_chip(planes))
    wires = Wires(send, recv)
    state = spread_start(wires, local, planes, lambda h, z: parcels.at[h, z], out)
    spread_finish(wires, planes, out, state)
    wires.sent()


def add_rows(target, others, rows):
    @pl.loop(0, rows // 16)
    def _(i):
        at = pl.ds(pl.multiple_of(i * 16, 16), 16)
        total = target[at, :].astype(jnp.float32)
        for other in others:
            total = total + other[at, :].astype(jnp.float32)
        target[at, :] = total.astype(target.dtype)


def scatter_steps(wires, local, planes, groups):
    h, z, c = place()
    row = 2 * z + c
    sib = (h, 2 * z + 1 - c)
    hx, hy, hd = across(h, 1), across(h, 2), across(h, 3)
    xn, yn = (hx, row), (hy, row)
    zs = [lax.rem(z + 1 + s, planes) for s in range(planes)]
    order = [(k, s) for k in range(len(groups)) for s in range(planes)]
    from_sib, loads = {}, {}
    for i, (k, s) in enumerate(order):
        grads, out, own, sibs, px, pz = groups[k]
        for q in (3, 1, 2, 0):
            th = across(h, q)
            from_sib[k, s, q] = wires.copy(grads.at[th, zs[s], 1 - c], sibs.at[th, zs[s]], sib)
        loads[k, s] = pltpu.make_async_copy(grads.at[:, zs[s], c], own.at[:, zs[s]], local.at[i])
        loads[k, s].start()
    first, second, from_z = {}, {}, {}

    def pair(k, s):
        grads, out, own, sibs, px, pz = groups[k]
        a, b = split(own.shape[2])
        loads[k, s].wait()
        for q in (3, 1, 2, 0):
            from_sib[k, s, q].wait_recv()
            th = across(h, q)
            add_rows(own.at[th, zs[s]], [sibs.at[th, zs[s]]], own.shape[2])
            if q == 3:
                first[k, s, "xd"] = wires.copy(
                    own.at[hd, zs[s]].at[a], px.at[zs[s], 0].at[a], xn
                )
                first[k, s, "yd"] = wires.copy(
                    own.at[hd, zs[s]].at[b], px.at[zs[s], 0].at[b], yn
                )
            if q == 1:
                first[k, s, "x"] = wires.copy(own.at[hx, zs[s]].at[a], px.at[zs[s], 1].at[a], xn)
            if q == 2:
                first[k, s, "y"] = wires.copy(own.at[hy, zs[s]].at[b], px.at[zs[s], 1].at[b], yn)

    def plane(k, s):
        grads, out, own, sibs, px, pz = groups[k]
        a, b = split(own.shape[2])
        first[k, s, "xd"].wait_recv()
        add_rows(own.at[hy, zs[s]].at[a], [px.at[zs[s], 0].at[a]], a.size)
        second[k, s, "y"] = wires.copy(own.at[hy, zs[s]].at[a], px.at[zs[s], 2].at[a], yn)
        first[k, s, "yd"].wait_recv()
        add_rows(own.at[hx, zs[s]].at[b], [px.at[zs[s], 0].at[b]], b.size)
        second[k, s, "x"] = wires.copy(own.at[hx, zs[s]].at[b], px.at[zs[s], 2].at[b], xn)

    def line(k, s):
        grads, out, own, sibs, px, pz = groups[k]
        for part in ("x", "y"):
            first[k, s, part].wait_recv()
            second[k, s, part].wait_recv()
        add_rows(own.at[h, zs[s]], [px.at[zs[s], 1], px.at[zs[s], 2]], own.shape[2])
        if s < planes - 1:
            from_z[k, s] = wires.copy(own.at[h, zs[s]], pz.at[s], (h, 2 * zs[s] + c))

    def total(k):
        grads, out, own, sibs, px, pz = groups[k]
        for s in range(planes - 1):
            from_z[k, s].wait_recv()

        @pl.loop(0, out.shape[0] // 16)
        def _(i):
            at = pl.ds(pl.multiple_of(i * 16, 16), 16)
            value = own[h, z, at, :].astype(jnp.float32)
            for s in range(planes - 1):
                value = value + pz[s, at, :].astype(jnp.float32)
            out[at, :] = value

    for i in range(len(order) + 2):
        if i < len(order):
            pair(*order[i])
        if 1 <= i <= len(order):
            plane(*order[i - 1])
        if i >= 2:
            line(*order[i - 2])
    for k in range(len(groups)):
        total(k)


def scatter_kernel(planes, count, *refs):
    grads, outs = refs[:count], refs[count : 2 * count]
    held = refs[2 * count : 2 * count + 4 * count]
    send, recv, local = refs[6 * count :]
    greet(near(planes))
    wires = Wires(send, recv)
    groups = [(grads[k], outs[k], *held[4 * k : 4 * k + 4]) for k in range(count)]
    scatter_steps(wires, local, planes, groups)
    wires.sent()


def give_kernel(planes, count, *refs):
    parcels, grads = refs[0], refs[1 : 1 + count]
    out, outs = refs[1 + count], refs[2 + count : 2 + 2 * count]
    held = refs[2 + 2 * count : 2 + 6 * count]
    mine, other, send, recv, local, extra = refs[2 + 6 * count :]
    greet(every_chip(planes))
    wires = Wires(send, recv)
    give_steps(wires, extra, planes, parcels, out, mine, other)
    groups = [(grads[k], outs[k], *held[4 * k : 4 * k + 4]) for k in range(count)]
    scatter_steps(wires, local, planes, groups)
    for one in wires.given:
        one.wait_recv()
    wires.sent()


def give_steps(wires, local, planes, parcels, out, mine, other):
    h, z, c = place()
    sib = (h, 2 * z + 1 - c)
    passed = wires.copy(parcels.at[1 - c], other, sib)
    load = pltpu.make_async_copy(parcels.at[c], mine, local.at[0])
    load.start()
    load.wait()
    passed.wait_recv()
    wires.given = []
    for q in (3, 1, 2, 0):
        for s in range(planes - 1, -1, -1):
            th, tz = across(h, q), lax.rem(z + s, planes)
            add_rows(mine.at[th, tz], [other.at[th, tz]], mine.shape[2])
            if q or s:
                wires.given.append(
                    wires.copy(mine.at[th, tz], out.at[h, z], (th, 2 * tz + c))
                )
    keep = pltpu.make_async_copy(mine.at[h, z], out.at[h, z], local.at[1])
    keep.start()
    keep.wait()


def return_kernel(planes, parcels, out, mine, other, send, recv, extra):
    greet(every_chip(planes))
    wires = Wires(send, recv)
    give_steps(wires, extra, planes, parcels, out, mine, other)
    for one in wires.given:
        one.wait_recv()
    wires.sent()


def params(number):
    return pltpu.CompilerParams(
        collective_id=number, has_side_effects=True, vmem_limit_bytes=56 << 20
    )


def dma(count):
    return pltpu.SemaphoreType.DMA((count,))


def gather_wires(planes, count):
    return count * (planes - 1 + planes * 8)


def spread_wires(planes):
    return 2 * 4 * planes


def scatter_wires(planes, count):
    return count * planes * 11


def held_scratch(planes, shape):
    rows, lanes = shape
    return [
        pltpu.VMEM((4, planes, rows, lanes), jnp.bfloat16),
        pltpu.VMEM((4, planes, rows, lanes), jnp.bfloat16),
        pltpu.VMEM((planes, 3, rows, lanes), jnp.bfloat16),
        pltpu.VMEM((planes - 1, rows, lanes), jnp.bfloat16),
    ]


class Kernels:
    def __init__(self, planes):
        self.planes = planes

    def ids(self, block):
        planes = self.planes
        wires = 2 * planes - 1
        return pl.pallas_call(
            functools.partial(ids_kernel, planes),
            out_shape=jax.ShapeDtypeStruct((2 * planes, *block.shape), block.dtype),
            in_specs=[ANY],
            out_specs=ANY,
            scratch_shapes=[dma(wires), dma(wires), pltpu.SemaphoreType.DMA],
            compiler_params=params(1),
            name="ids",
        )(block)

    def fetch(self, parcels, blocks):
        planes, count = self.planes, len(blocks)
        wires = gather_wires(planes, count) + spread_wires(planes)
        result = pl.pallas_call(
            functools.partial(fetch_kernel, planes, count),
            out_shape=[jax.ShapeDtypeStruct((2, *parcels.shape), parcels.dtype)]
            + [jax.ShapeDtypeStruct((4, planes, 2, *b.shape), b.dtype) for b in blocks],
            in_specs=[ANY] * (1 + count),
            out_specs=[ANY] * (1 + count),
            scratch_shapes=[dma(wires), dma(wires), dma(count + 1)],
            compiler_params=params(2),
            name="fetch",
        )(parcels, *blocks)
        return result[0], result[1:]

    def deliver(self, parcels):
        planes = self.planes
        wires = spread_wires(planes)
        return pl.pallas_call(
            functools.partial(deliver_kernel, planes),
            out_shape=jax.ShapeDtypeStruct((2, *parcels.shape), parcels.dtype),
            in_specs=[ANY],
            out_specs=ANY,
            scratch_shapes=[dma(wires), dma(wires), pltpu.SemaphoreType.DMA],
            compiler_params=params(3),
            name="deliver",
        )(parcels)

    def rows(self, block):
        planes = self.planes
        wires = gather_wires(planes, 1)
        return pl.pallas_call(
            functools.partial(gather_kernel, planes, 1),
            out_shape=jax.ShapeDtypeStruct((4, planes, 2, *block.shape), block.dtype),
            in_specs=[ANY],
            out_specs=ANY,
            scratch_shapes=[dma(wires), dma(wires), dma(1)],
            compiler_params=params(4),
            name="rows",
        )(block)

    def small(self, block, number):
        planes = self.planes
        wires = spread_wires(planes)
        return pl.pallas_call(
            functools.partial(small_kernel, planes),
            out_shape=jax.ShapeDtypeStruct((2, 4, planes, *block.shape), block.dtype),
            in_specs=[VMEM],
            out_specs=VMEM,
            scratch_shapes=[dma(wires), dma(wires), pltpu.SemaphoreType.DMA],
            compiler_params=params(number),
            name="small",
        )(block)

    def scatter_rows(self, grads):
        planes = self.planes
        shape = grads.shape[3:]
        wires = scatter_wires(planes, 1)
        return pl.pallas_call(
            functools.partial(scatter_kernel, planes, 1),
            out_shape=jax.ShapeDtypeStruct(shape, jnp.float32),
            in_specs=[ANY],
            out_specs=VMEM,
            scratch_shapes=held_scratch(planes, shape) + [dma(wires), dma(wires), dma(planes)],
            compiler_params=params(7),
            name="scatter_rows",
        )(grads)

    def give(self, parcels, grads):
        planes, count = self.planes, len(grads)
        shapes = [g.shape[3:] for g in grads]
        wires = scatter_wires(planes, count) + spread_wires(planes)
        held = [s for shape in shapes for s in held_scratch(planes, shape)]
        layer = parcels.shape[1:]
        result = pl.pallas_call(
            functools.partial(give_kernel, planes, count),
            out_shape=[jax.ShapeDtypeStruct(layer, parcels.dtype)]
            + [jax.ShapeDtypeStruct(shape, jnp.float32) for shape in shapes],
            in_specs=[ANY] * (1 + count),
            out_specs=[ANY] + [VMEM] * count,
            scratch_shapes=held
            + [pltpu.VMEM(layer, parcels.dtype), pltpu.VMEM(layer, parcels.dtype)]
            + [dma(wires), dma(wires), dma(planes * count), dma(2)],
            compiler_params=params(8),
            name="give",
        )(parcels, *grads)
        return result[0], result[1:]

    def hand_back(self, parcels):
        planes = self.planes
        layer = parcels.shape[1:]
        wires = spread_wires(planes)
        return pl.pallas_call(
            functools.partial(return_kernel, planes),
            out_shape=jax.ShapeDtypeStruct(layer, parcels.dtype),
            in_specs=[ANY],
            out_specs=ANY,
            scratch_shapes=[pltpu.VMEM(layer, parcels.dtype), pltpu.VMEM(layer, parcels.dtype)]
            + [dma(wires), dma(wires), dma(2)],
            compiler_params=params(9),
            name="hand_back",
        )(parcels)


class Plain:
    def __init__(self, planes):
        self.planes = planes

    def ids(self, block):
        return lax.all_gather(block, "row")

    def gather(self, block):
        whole = lax.all_gather(block, ("head", "row"))
        return whole.reshape(4, self.planes, 2, *block.shape)

    def fetch(self, parcels, blocks):
        return self.deliver(parcels), [self.gather(b) for b in blocks]

    def deliver(self, parcels):
        shape = parcels.shape
        both = jnp.broadcast_to(parcels[:, :, None], (*shape[:2], 2, *shape[2:]))
        flat = both.reshape(8 * self.planes, *shape[2:])
        got = lax.all_to_all(flat, ("head", "row"), split_axis=0, concat_axis=0, tiled=True)
        return jnp.moveaxis(got.reshape(4, self.planes, 2, *shape[2:]), 2, 0)

    def rows(self, block):
        return self.gather(block)

    def small(self, block, number):
        return jnp.moveaxis(self.gather(block), 2, 0)

    def scatter_rows(self, grads):
        flat = grads.reshape(-1, grads.shape[-1]).astype(jnp.float32)
        return lax.psum_scatter(flat, ("head", "row"), scatter_dimension=0, tiled=True)

    def give(self, parcels, grads):
        return self.hand_back(parcels), [self.scatter_rows(g) for g in grads]

    def hand_back(self, parcels):
        shape = parcels.shape
        flat = jnp.moveaxis(parcels, 0, 2).reshape(8 * self.planes, *shape[3:])
        got = lax.all_to_all(flat, ("head", "row"), split_axis=0, concat_axis=0, tiled=True)
        got = got.reshape(4, self.planes, 2, *shape[3:]).astype(jnp.float32)
        return jnp.sum(got, axis=2).astype(parcels.dtype)


def contract(left, right, left_dim, right_dim):
    return lax.dot_general(
        left, right, (((left_dim,), (right_dim,)), ((), ())), preferred_element_type=jnp.float32
    )


def normalize(values, gain, shift):
    center = values - jnp.mean(values, axis=-1, keepdims=True)
    scale = lax.rsqrt(jnp.mean(center * center, axis=-1, keepdims=True) + EPSILON)
    unit = center * scale
    return (unit * gain + shift, unit, scale)


def normalize_back(grad, unit, scale, gain):
    inner = grad * gain
    back = scale * (
        inner
        - jnp.mean(inner, axis=-1, keepdims=True)
        - unit * jnp.mean(inner * unit, axis=-1, keepdims=True)
    )
    return (back, grad * unit)


def score_block(query, keys, labels):
    scores = jnp.einsum("qhe,khe->hqk", query, keys, preferred_element_type=jnp.float32) * HD ** (
        -0.5
    )
    allowed = labels[:, None] == labels[None, :]
    return jnp.where(allowed[None], scores, -1000000000.0)


def attend_fwd(query, keys, values, labels):
    scores = score_block(query, keys, labels)
    top = jnp.max(scores, axis=-1, keepdims=True)
    weights = jnp.exp(scores - top)
    total = jnp.sum(weights, axis=-1, keepdims=True)
    probs = weights / total
    output = jnp.einsum(
        "hqk,khe->qhe", probs.astype(jnp.bfloat16), values, preferred_element_type=jnp.float32
    )
    return (output, (top + jnp.log(total))[..., 0])


def attend_back(query, keys, values, labels, summary, grad_out):
    scores = score_block(query, keys, labels)
    probs = jnp.exp(scores - summary[..., None])
    grad_values = jnp.einsum(
        "hqk,qhe->khe", probs.astype(jnp.bfloat16), grad_out, preferred_element_type=jnp.float32
    )
    grad_probs = jnp.einsum("qhe,khe->hqk", grad_out, values, preferred_element_type=jnp.float32)
    grad_scores = probs * (grad_probs - jnp.sum(grad_probs * probs, axis=-1, keepdims=True))
    grad_low = grad_scores.astype(jnp.bfloat16)
    grad_query = jnp.einsum(
        "hqk,khe->qhe", grad_low, keys, preferred_element_type=jnp.float32
    ) * HD ** (-0.5)
    grad_keys = jnp.einsum(
        "hqk,qhe->khe", grad_low, query, preferred_element_type=jnp.float32
    ) * HD ** (-0.5)
    return jnp.stack([grad_query, grad_keys, grad_values], axis=2)


def adamw(weight, grad, first, second, decay, rate):
    first = BETA_ONE * first + (1 - BETA_ONE) * grad
    second = BETA_TWO * second + (1 - BETA_TWO) * grad * grad
    moved = first / (1 - BETA_ONE**STEP) / (jnp.sqrt(second / (1 - BETA_TWO**STEP)) + ADAM_EPSILON)
    return (weight - rate * (moved + decay * weight), first, second)


def padded(flat, rows, lanes):
    return jnp.pad(flat, (0, rows * lanes - flat.shape[0])).reshape(rows, lanes)


def on_device(
    token_ids,
    segment_ids,
    masked_pos,
    masked_target,
    embedding,
    position_table,
    qkv_weight,
    out_weight,
    up_weight,
    down_weight,
    norm_params,
    up_bias,
    m_embedding,
    m_position,
    m_qkv,
    m_out,
    m_up,
    m_down,
    m_norm,
    m_bias,
    v_embedding,
    v_position,
    v_qkv,
    v_out,
    v_up,
    v_down,
    v_norm,
    v_bias,
):
    low = jnp.bfloat16
    row_count = lax.axis_size("row")
    devices = HEADS * row_count
    planes = row_count // 2
    wire = Kernels(planes) if planes <= 4 else Plain(planes)
    head = lax.axis_index("head")
    row = lax.axis_index("row")
    core = row % 2
    device = head * row_count + row
    vocab_part, width = embedding.shape
    tokens = token_ids.shape[0] // HEADS
    inner = up_weight.shape[1] * devices

    labels_all = segment_ids.reshape(HEADS, tokens)
    slots = masked_pos.shape[1] // HEADS
    live = labels_at(segment_ids, masked_pos[0])
    target = jnp.where(live, masked_target[0], -1)
    words = token_ids.shape[0] + target.shape[0]
    lines = -(-words // 1024) * 8
    numbers = wire.ids(padded(jnp.concatenate([token_ids, target]), lines, 128))
    numbers = numbers.reshape(row_count, lines * 128)
    ids = numbers[:, : token_ids.shape[0]].reshape(planes, 2, HEADS, tokens)
    ids = ids.transpose(2, 0, 1, 3).reshape(HEADS * planes, 2 * tokens)
    targets = numbers[:, token_ids.shape[0] : words].reshape(row_count, HEADS, slots)
    targets = targets.transpose(1, 0, 2).reshape(-1)

    owner = ids // vocab_part
    counts = jnp.sum(owner[:, :, None] == jnp.arange(devices), axis=1)
    rounds = -(-jnp.max(counts) // ROOM)
    inside = owner == device
    order = jnp.arange(2 * tokens)
    before = (order[:, None] < order[None, :]).astype(low)
    rank = jnp.dot(inside.astype(low), before, preferred_element_type=jnp.float32).astype(jnp.int32)
    rank = jnp.where(inside, rank, -1)
    local = ids - device * vocab_part
    chip = head * planes + row // 2
    own_owner = lax.dynamic_index_in_dim(owner, chip, 0, keepdims=False)
    own_marks = own_owner[:, None] == jnp.arange(devices)
    own_before = contract(before, own_marks.astype(low), 0, 0).astype(jnp.int32)
    own_rank = jnp.sum(jnp.where(own_marks, own_before, 0), axis=1)
    own_owner = lax.dynamic_slice_in_dim(own_owner, core * tokens, tokens, 0)
    own_rank = lax.dynamic_slice_in_dim(own_rank, core * tokens, tokens, 0)
    own_home = (own_owner % 2) * (devices // 2) + own_owner // 2
    table = embedding.astype(low)

    def parcel_marks(turn):
        spot = jnp.arange(ROOM) + turn * ROOM
        hit = rank[:, None, :] == spot[None, :, None]
        which = jnp.sum(jnp.where(hit, local[:, None, :] + 1, 0), axis=2) - 1
        marks = which.reshape(-1)[:, None] == jnp.arange(vocab_part)[None, :]
        return marks.astype(low)

    def token_marks(turn):
        seat = own_rank - turn * ROOM
        seat = jnp.where((seat >= 0) & (seat < ROOM), own_home * ROOM + seat, -1)
        return (seat[:, None] == jnp.arange(devices * ROOM)[None, :]).astype(low)

    def parcels_of(turn):
        picked = jnp.dot(parcel_marks(turn), table, preferred_element_type=jnp.float32)
        return picked.astype(low).reshape(HEADS, planes, ROOM, width)

    def opened(parcels, turn):
        return jnp.dot(
            token_marks(turn),
            parcels.reshape(devices * ROOM, width),
            preferred_element_type=jnp.float32,
        )

    share = width // devices
    share_inner = inner // devices
    misc = jnp.concatenate(
        [
            out_weight.T.reshape(-1),
            position_table.T.reshape(-1),
            norm_params.reshape(-1),
            up_bias,
        ]
    ).astype(low)
    misc_rows = -(-misc.shape[0] // (16 * width)) * 16
    parcels, gathered = wire.fetch(
        parcels_of(0),
        [
            padded(misc, misc_rows, width),
            qkv_weight.astype(low),
            up_weight.T.astype(low),
            down_weight.astype(low),
        ],
    )
    looked = opened(parcels, 0)

    def again(state):
        turn, so_far = state
        return turn + 1, so_far + opened(wire.deliver(parcels_of(turn)), turn)

    _, looked = lax.while_loop(lambda state: state[0] < rounds, again, (jnp.int32(1), looked))

    misc_all = gathered[0].reshape(devices, misc_rows * width)
    qkv_full = gathered[1].reshape(HEADS, width, qkv_weight.shape[1])
    up_full = gathered[2].reshape(inner, width)
    down_full = gathered[3].reshape(inner, width)
    cuts = [share * width, share * SEQ, share * 8, share_inner]
    starts = [sum(cuts[:i]) for i in range(5)]
    pieces = [misc_all[:, starts[i] : starts[i + 1]] for i in range(4)]
    out_full = pieces[0].reshape(width, width)
    places = pieces[1].reshape(width, SEQ).T
    norms = pieces[2].reshape(devices, 8, share).transpose(1, 0, 2).reshape(8, width)
    norms = norms.astype(jnp.float32)
    bias = pieces[3].reshape(inner).astype(jnp.float32)

    labels = lax.dynamic_index_in_dim(labels_all, head, 0, keepdims=False)
    start_sum = looked + places.astype(jnp.float32)
    normed, unit_zero, scale_zero = normalize(start_sum, norms[0], norms[1])
    normed_low = normed.astype(low)
    mixed = jnp.einsum("td,hdj->thj", normed_low, qkv_full, preferred_element_type=jnp.float32)
    mixed = mixed.astype(low).reshape(tokens, -1, 3, HD)
    heads = mixed.shape[1]
    query, keys, values = (mixed[:, :, 0], mixed[:, :, 1], mixed[:, :, 2])
    attended, summary = attend_fwd(query, keys, values, labels)
    head_ramp = jnp.where(jnp.arange(heads) < OLD_HEADS, 1.0, STEP / RAMP).astype(jnp.float32)
    heads_low = (attended * head_ramp[:, None]).astype(low).reshape(tokens, heads * HD)
    projected = contract(heads_low, out_full, 1, 1)
    hidden, unit_one, scale_one = normalize(normed + projected + norms[6], norms[2], norms[3])
    hidden_low = hidden.astype(low)
    upper = contract(hidden_low, up_full, 1, 1) + bias
    neuron_ramp = jnp.where(jnp.arange(inner) < OLD_FF, 1.0, STEP / RAMP).astype(jnp.float32)
    activated, gelu_pull = jax.vjp(
        lambda u: jax.nn.gelu(u, approximate=False) * neuron_ramp, upper
    )
    active_low = activated.astype(low)
    lowered = jnp.dot(active_low, down_full, preferred_element_type=jnp.float32) + norms[7]
    final, unit_two, scale_two = normalize(hidden + lowered, norms[4], norms[5])

    chosen = lax.dynamic_slice_in_dim(masked_pos[0], head * slots, slots, 0) - head * tokens
    chosen_marks = chosen[:, None] == jnp.arange(tokens)[None, :]
    picked = jnp.dot(chosen_marks.astype(low), final.astype(low), preferred_element_type=jnp.float32)
    all_rows = wire.rows(picked.astype(low)).reshape(devices * slots, width)
    valid = (targets >= 0).astype(jnp.float32)
    logits = contract(all_rows, table, 1, 1)
    hits = jnp.arange(vocab_part)[None, :] == (targets - device * vocab_part)[:, None]
    top = jnp.max(logits, axis=1)
    part = top + jnp.log(jnp.sum(jnp.exp(logits - top[:, None]), axis=1))
    parts = wire.small(part.reshape(-1, 128), 5).reshape(devices, -1)
    peak = jnp.max(parts, axis=0)
    log_total = peak + jnp.log(jnp.sum(jnp.exp(parts - peak), axis=0))
    target_part = jnp.sum(jnp.where(hits, logits, 0.0))
    log_own = lax.dynamic_slice_in_dim(log_total * valid, device * slots, slots, 0)
    valid_own = lax.dynamic_slice_in_dim(valid, device * slots, slots, 0)
    loss_own = jnp.sum(log_own) - target_part
    count_own = jnp.sum(valid_own)
    grad_logits = (
        valid[:, None] * (jnp.exp(logits - log_total[:, None]) - hits.astype(jnp.float32))
    ).astype(low)
    grad_table = contract(grad_logits, all_rows, 0, 0)
    grad_rows = jnp.dot(grad_logits, table, preferred_element_type=jnp.float32).astype(low)
    grad_picked = wire.scatter_rows(grad_rows.reshape(HEADS, planes, 2, slots, width))

    grad_final = lax.dot_general(
        chosen_marks.astype(jnp.float32),
        grad_picked,
        (((0,), (0,)), ((), ())),
        precision=lax.Precision.HIGHEST,
    )
    grad_sum, gain_two = normalize_back(grad_final, unit_two, scale_two, norms[4])
    grad_sum_low = grad_sum.astype(low)
    grad_down = contract(active_low, grad_sum_low, 0, 0)
    grad_upper = gelu_pull(contract(grad_sum_low, down_full, 1, 1))[0]
    grad_upper_low = grad_upper.astype(low)
    grad_up = contract(grad_upper_low, hidden_low, 0, 0)
    grad_hidden = grad_sum + jnp.dot(grad_upper_low, up_full, preferred_element_type=jnp.float32)
    grad_res, gain_one = normalize_back(grad_hidden, unit_one, scale_one, norms[2])
    grad_res_low = grad_res.astype(low)
    grad_out = contract(grad_res_low, heads_low, 0, 0)
    grad_heads = jnp.dot(grad_res_low, out_full, preferred_element_type=jnp.float32).astype(low)
    grad_attended = (
        grad_heads.reshape(tokens, heads, HD).astype(jnp.float32) * head_ramp[:, None]
    ).astype(low)
    grad_mixed = attend_back(query, keys, values, labels, summary, grad_attended)
    grad_mixed_low = grad_mixed.astype(low).reshape(tokens, HEADS, -1)
    grad_qkv = jnp.einsum(
        "td,thj->hdj", normed_low, grad_mixed_low, preferred_element_type=jnp.float32
    )
    grad_normed = grad_res + jnp.einsum(
        "thj,hdj->td", grad_mixed_low, qkv_full, preferred_element_type=jnp.float32
    )
    grad_start, gain_zero = normalize_back(grad_normed, unit_zero, scale_zero, norms[0])
    grad_start_low = grad_start.astype(low)
    grad_norms = jnp.stack(
        [
            jnp.sum(gain_zero, axis=0),
            jnp.sum(grad_normed, axis=0),
            jnp.sum(gain_one, axis=0),
            jnp.sum(grad_hidden, axis=0),
            jnp.sum(gain_two, axis=0),
            jnp.sum(grad_final, axis=0),
            jnp.sum(grad_res, axis=0),
            jnp.sum(grad_sum, axis=0),
        ]
    )
    grad_bias = jnp.sum(grad_upper, axis=0)

    def parcels_back(turn):
        back = contract(token_marks(turn), grad_start_low, 0, 0).astype(low)
        return back.reshape(2, HEADS, planes, ROOM, width)

    def unpacked(parcels, turn):
        return contract(parcel_marks(turn), parcels.reshape(-1, width), 0, 0)

    grad_misc = jnp.concatenate(
        [
            grad_out.reshape(devices, -1),
            grad_start.T.reshape(devices, -1),
            grad_norms.reshape(8, devices, share).transpose(1, 0, 2).reshape(devices, -1),
            grad_bias.reshape(devices, -1),
        ],
        axis=1,
    ).astype(low)
    grad_misc = jnp.pad(grad_misc, ((0, 0), (0, misc_rows * width - grad_misc.shape[1])))
    parcels, summed = wire.give(
        parcels_back(0),
        [
            grad_misc.reshape(HEADS, planes, 2, misc_rows, width),
            grad_qkv.astype(low).reshape(HEADS, planes, 2, *qkv_weight.shape),
            grad_up.astype(low).reshape(HEADS, planes, 2, share_inner, width),
            grad_down.astype(low).reshape(HEADS, planes, 2, share_inner, width),
        ],
    )
    grad_table = grad_table + unpacked(parcels, 0)

    def again_back(state):
        turn, so_far = state
        return turn + 1, so_far + unpacked(wire.hand_back(parcels_back(turn)), turn)

    _, grad_table = lax.while_loop(
        lambda state: state[0] < rounds, again_back, (jnp.int32(1), grad_table)
    )
    misc_sum = summed[0].reshape(-1)
    grads = (
        grad_table,
        misc_sum[starts[1] : starts[2]].reshape(share, SEQ).T,
        summed[1],
        misc_sum[starts[0] : starts[1]].reshape(share, width).T,
        summed[2].T,
        summed[3],
        misc_sum[starts[2] : starts[3]].reshape(8, share),
        misc_sum[starts[3] : starts[4]],
    )
    squares = sum((jnp.sum(g * g) for g in grads))
    scalars = padded(jnp.stack([squares, loss_own, count_own]), 8, 128)
    scalars = jnp.sum(wire.small(scalars, 6).reshape(devices, 8, 128)[:, 0, :3], axis=0)
    squares, loss_sum, live_count = scalars[0], scalars[1], scalars[2]
    grad_norm = jnp.sqrt(squares) / live_count
    factor = jnp.minimum(1.0, CLIP / grad_norm) / live_count
    weights = (
        embedding,
        position_table,
        qkv_weight,
        out_weight,
        up_weight,
        down_weight,
        norm_params,
        up_bias,
    )
    firsts = (m_embedding, m_position, m_qkv, m_out, m_up, m_down, m_norm, m_bias)
    seconds = (v_embedding, v_position, v_qkv, v_out, v_up, v_down, v_norm, v_bias)
    decays = (DECAY,) * 6 + (0.0, 0.0)
    rates = (LEARN_RATE,) * 6 + (GAIN_RATE,) * 2
    results = [
        adamw(w, g * factor, m, v, d, r)
        for w, g, m, v, d, r in zip(weights, grads, firsts, seconds, decays, rates)
    ]
    return (
        *(r[0] for r in results),
        *(r[1] for r in results),
        *(r[2] for r in results),
        loss_sum,
        live_count,
        grad_norm,
    )


def labels_at(segment_ids, positions):
    at = positions[:, None] == jnp.arange(segment_ids.shape[0])[None, :]
    return jnp.sum(jnp.where(at, segment_ids[None, :], 0), axis=1) != SEQ - 1


def solution(mesh):
    vocab = P(("head", "row"), None)
    columns = P(None, ("head", "row"))
    flat = P(("head", "row"))
    weights = (vocab, columns, P("row", "head"), columns, columns, vocab, columns, flat)
    data = (P("row"), P("row"), P("row", None), P("row", None))
    return jax.shard_map(
        on_device,
        mesh=mesh,
        in_specs=(*data, *weights, *weights, *weights),
        out_specs=(*weights, *weights, *weights, P(), P(), P()),
        check_vma=False,
    )
```

time: 1380 us -> 586 us (0.42)
  waiting for transfers between devices: 775 us -> 0 us
  Pallas kernels: 0 us -> 314 us
  blocking collectives: 256 us -> 0 us
  other arithmetic: 122 us -> 68.6 us
    reduce_scatter x6 -> x0, waiting for transfers between devices: 535 us -> none  [the longest x1 232 us: on_device(): lax.psum_scatter(grad_table, 'row', scatter_dimension=0, tiled=True)]
    pallas_call x0 -> x7, Pallas kernels: none -> 314 us  [the longest x1 135 us: fetch(): pl.pallas_call(functools.partial(fetch_kernel, planes, count), out_shape=...]
    all_gather x7 -> x0, blocking collectives: 132 us -> none  [the longest x1 43 us: on_device(): lax.all_gather(position_table.astype(jnp.bfloat16), ('head', 'row'), axis...]
    all_gather x4 -> x0, waiting for transfers between devices: 112 us -> none  [the longest x1 112 us: on_device(): lax.all_gather(embedding.astype(jnp.bfloat16), 'row', axis=0, tiled=True)]
    unnamed x2 -> x0, blocking collectives: 85.9 us -> none
    psum x2 -> x0, waiting for transfers between devices: 75.3 us -> none  [the longest x1 75.3 us: on_device(): lax.psum(grad_input.astype(jnp.bfloat16), 'head').astype(jnp.float32)]
    unnamed x14 -> x0, waiting for transfers between devices: 41.1 us -> none
    psum x1 -> x0, blocking collectives: 38.3 us -> none  [on_device(): lax.psum((squares, loss_own, count_own), ('head', 'row'))]
  transfers between devices with their start and end apart: 15 -> 0, of which waited for: 8 -> 0; matrix products, arithmetic and copies ran while one was open for 12% -> 0% of each run, Pallas kernels for 0% -> 0%
where the time goes in v1:
time: 586 us; the launch traced here: 577 us
  Pallas kernels  314 us (54%)
  matrix products  139 us (24%)
  other arithmetic  68.6 us (12%)
  local copies, waits for them, and re-layouts  40.9 us (7%)
  between operations  14.1 us (2%)
    pallas_call x1, Pallas kernels, fetch(): pl.pallas_call(functools.partial(fetch_kernel, planes, count), out_shape=...  135 us
    pallas_call x1, Pallas kernels, give(): pl.pallas_call(functools.partial(give_kernel, planes, count), out_shape=[...  101 us
    dot_general x11, matrix products, contract(): lax.dot_general(left, right, (((left_dim,), (right_dim,)), ((), ())), pre...  74.2 us
    pallas_call x1, Pallas kernels, scatter_rows(): pl.pallas_call(functools.partial(scatter_kernel, planes, 1), out_shape=ja...  23.6 us
    pallas_call x1, Pallas kernels, rows(): pl.pallas_call(functools.partial(gather_kernel, planes, 1), out_shape=jax...  23.4 us
    pallas_call x2, Pallas kernels, small(): pl.pallas_call(functools.partial(small_kernel, planes), out_shape=jax.Sha...  21.7 us
    sub x8, other arithmetic, adamw(): return (weight - rate * (moved + decay * weight), first, second)  18.3 us
    reduce_sum x8, other arithmetic, on_device(): squares = sum((jnp.sum(g * g) for g in grads))  11.8 us

profile of v1, /device:TPU:0, one launch (start us, length us, event | category | flops | bytes accessed | tf_op | source)
XLA Modules:
  0.0 576.8 jit_solution(5951896776329269325)
XLA Ops:
  9.3 8.5 %ids.1 = s32[8,24,128]{2,1,0:T(8,128)} custom-call(s32[24,128]{1,0:T(8,128)} %pad_bitcast_fusion.x), custom_call_target="tpu_custom_call" | custom-call | tf_op jit(solution)/shard_map/ids/pallas_call | solution.py:433
  32.2 135.5 %fetch.1 = (bf16[2,4,4,64,768]{4,3,2,1,0:T(8,128)(2,1)}, bf16[4,4,2,48,768]{4,3,2,1,0:T(8,128)(2,1)}, bf16[4,4,2,96,576]{4,3,2,1,0:T(8,128)(2,1)}, bf16[4,4,2,96...) custom-call(bf16[4,4,64,768]{3,2,1,0:T(8,128)(2,1)} %bitcast.226, bf16[48,768]{1,0:T(8,128)(2,1)} %reshape.564.refs_1_, ...), custom_call_target="tpu_custom_call" | custom-call | tf_op jit(solution)/shard_map/fetch/pallas_call | solution.py:446
  167.7 5.1 fusion.28
  195.1 4.8 multiply_convert_fusion.5
  201.5 27.7 %multiply_convert_fusion.2 = (bf16[512,3072]{1,0:T(8,128)(2,1)S(1)}, f32[512,3072]{1,0:T(8,128)}, f32[512,3072]{1,0:T(8,128)}) fusion(f32[3072]{0:T(1024)S(1)} %fusion.82, f32[3072]{0:T(1024)S(1)} %reshape.590, bf16[3072,768]{1,0:T(8,128)(2,1)} %bitcast.251, f32[512,768]{1,0:T(8,128)S(1)} %get-tuple-element.354, f32[768]{0:T(1024)S(1)} %add.472, ...), kind=kOutput, calls=%fused_computation.43 | convolution fusion | flops 2523267072 | bytes 22054912 | tf_op jit(solution)/shard_map/dot_general | solution.py:590
  234.3 23.4 %rows.1 = bf16[4,4,2,64,768]{4,3,2,1,0:T(8,128)(2,1)} custom-call(bf16[64,768]{1,0:T(8,128)(2,1)} %convolution_convert_fusion.6.refs_0_), custom_call_target="tpu_custom_call" | custom-call | tf_op jit(solution)/shard_map/rows/pallas_call | solution.py:474
  257.8 5.1 fusion.122
  266.6 11.4 %small.2 = f32[2,4,4,16,128]{4,3,2,1,0:T(8,128)} custom-call(f32[16,128]{1,0:T(8,128)} %add_bitcast_fusion.1.x), custom_call_target="tpu_custom_call" | custom-call | tf_op jit(solution)/shard_map/small/pallas_call | solution.py:487
  280.1 10.2 %fusion.99 = f32[960,768]{1,0:T(8,128)} fusion(bf16[2048,768]{1,0:T(8,128)(2,1)} %bitcast.220, f32[2048,960]{0,1:T(8,128)} %copy-done.9, s32[2048]{0:T(1024)S(1)} %copy-done.39, f32[2048]{0:T(1024)S(1)} %add_bitcast_fusion, f32[2048]{0:T(1024)S(1)} %copy-done.42), kind=kOutput, calls=%fused_computation.284 | convolution fusion | flops 3031695360 | bytes 13983744 | tf_op jit(solution)/shard_map/dot_general | solution.py:590
  290.3 5.9 %convolution_convert_fusion.2 = bf16[2048,768]{1,0:T(8,128)(2,1)} fusion(bf16[960,768]{1,0:T(8,128)(2,1)S(1)} %copy-done.28, f32[2048,960]{0,1:T(8,128)S(1)} %copy-done.10, s32[2048]{0:T(1024)S(1)} %copy-done.39, f32[2048]{0:T(1024)S(1)} %add_bitcast_fusion, f32[2048]{0:T(1024)S(1)} %copy-done.42), kind=kOutput, calls=%fused_computation.75 | convolution fusion | flops 3033268224 | bytes 12509184 | tf_op jit(solution)/shard_map/dot_general | solution.py:844
  298.8 23.6 %scatter_rows.1 = f32[64,768]{1,0:T(8,128)} custom-call(bf16[4,4,2,64,768]{4,3,2,1,0:T(8,128)(2,1)} %bitcast.221), custom_call_target="tpu_custom_call" | custom-call | tf_op jit(solution)/shard_map/scatter_rows/pallas_call | solution.py:501
  325.4 9.4 %fusion.123 = (bf16[3072]{0:T(1024)(128)(2,1)S(1)}, bf16[512,3072]{1,0:T(8,128)(2,1)S(1)}) fusion(f32[512,3072]{1,0:T(8,128)} %get-tuple-element.340, f32[3072]{0:T(1024)S(1)} %fusion.82, bf16[3072,768]{1,0:T(8,128)(2,1)} %bitcast.255, f32[512,768]{1,0:T(8,128)S(1)} %get-tuple-element.336, f32[512,3072]{1,0:T(8,128)} %get-tuple-element.355, ...), kind=kOutput, calls=%fused_computation.293 | convolution fusion | flops 2443047936 | bytes 22050816 | tf_op jit(solution)/shard_map/dot_general | solution.py:590
  337.9 4.4 convolution_convert_fusion
  342.8 4.7 convolution_convert_fusion.1
  359.7 8.4 %fusion.42 = bf16[512,12,1,64]{0,3,1,2:T(8,128)(2,1)S(1)} fusion(f32[12,512]{1,0:T(8,128)S(1)} %log_add_fusion, f32[12,512,512]{1,2,0:T(8,128)} %copy-done, pred[512,512]{0,1:T(8,128)(4,1)S(1)} %broadcast_compare_fusion, f32[512,12,64]{0,2,1:T(8,128)} %bitcast.214, f32[12]{0:T(128)S(1)} %compare_select_fusion), kind=kOutput, calls=%fused_computation.119 | convolution fusion | flops 416022528 | bytes 15228976 | tf_op jit(solution)/shard_map/hqk,qhe->khe/dot_general | solution.py:635
  368.2 9.9 %multiply_reduce_fusion = (f32[12,512]{1,0:T(8,128)S(1)}, f32[12,512,512]{1,2,0:T(8,128)}) fusion(f32[12,512]{1,0:T(8,128)S(1)} %log_add_fusion, f32[12,512,512]{1,2,0:T(8,128)} %copy-done, pred[512,512]{0,1:T(8,128)(4,1)S(1)} %broadcast_compare_fusion, bf16[512,12,3,64]{0,3,2,1:T(8,128)(2,1)S(1)} %bitcast.207, f32[512,12,64]{0,2,1:T(8,128)S(1)} %bitcast.215, ...), kind=kOutput, calls=%fused_computation.27 | convolution fusion | flops 419162112 | bytes 27845120 | tf_op jit(solution)/shard_map/qhe,khe->hqk/dot_general | solution.py:638
  378.1 7.0 %multiply_convert_fusion = bf16[12,512,512]{1,2,0:T(8,128)(2,1)S(1)} fusion(f32[12,512,512]{1,2,0:T(8,128)} %get-tuple-element.363, f32[12,512]{1,0:T(8,128)S(1)} %get-tuple-element.362, f32[12,512]{1,0:T(8,128)S(1)} %log_add_fusion, f32[12,512,512]{1,2,0:T(8,128)S(1)} %bitcast.195, pred[512,512]{0,1:T(8,128)(4,1)S(1)} %broadcast_compare_fusion), kind=kLoop, calls=%fused_computation.26 | loop fusion | flops 18874368 | bytes 31768576 | tf_op jit(solution)/shard_map/convert_element_type | solution.py:640
  394.9 4.0 convert_bitcast_fusion
  399.3 6.0 %copy.125 = bf16[4,768,576]{2,1,0:T(8,128)(2,1)} copy(bf16[4,768,576]{1,2,0:T(8,128)(2,1)} %convert_bitcast_fusion) | data formatting | bytes 7077888 | tf_op jit(solution)/shard_map/convert_element_type | solution.py:912
  411.4 3.6 fusion.31
  415.0 101.2 %give.1 = (bf16[4,4,64,768]{3,2,1,0:T(8,128)(2,1)}, f32[48,768]{1,0:T(8,128)}, f32[96,576]{1,0:T(8,128)}, f32[96,768]{1,0:T(8,128)}, f32[96,768]{1,0:T(8,128)}) custom-call(bf16[2,4,4,64,768]{4,3,2,1,0:T(8,128)(2,1)} %bitcast.218, bf16[4,4,2,48,768]{4,3,2,1,0:T(8,128)(2,1)} %bitcast.201, bf16[4,4,2,96,576]{4,3,2,1,0:T(8,128)(2,1)} %bitcast.200, ...), custom_call_target="tpu_custom_call" | custom-call | tf_op jit(solution)/shard_map/give/pallas_call | solution.py:517
  524.1 4.5 fusion.38
  541.6 10.3 %small.3 = f32[2,4,4,8,128]{4,3,2,1,0:T(8,128)} custom-call(f32[8,128]{1,0:T(8,128)} %fusion.84.x), custom_call_target="tpu_custom_call" | custom-call | tf_op jit(solution)/shard_map/small/pallas_call | solution.py:487
  569.6 5.6 multiply_subtract_fusion
  (298 shorter events, 122.4 us)
Async XLA Ops:
  8.6 19.4 %copy-start.29 = (f32[96,768]{1,0:T(8,128)S(1)}, f32[96,768]{1,0:T(8,128)}, u32[]{:S(2)}) copy-start(f32[96,768]{1,0:T(8,128)} %param.41) | copy-start | bytes 884740
  21.2 146.4 %copy-start.49 = (s32[512]{0:T(512)}, s32[512]{0:T(512)S(1)}, u32[]{:S(2)}) copy-start(s32[512]{0:T(512)S(1)} %get-tuple-element.343) | copy-start | bytes 6148
  175.0 25.0 %copy-start.47 = (f32[768]{0:T(1024)}, f32[768]{0:T(1024)S(1)}, u32[]{:S(2)}) copy-start(f32[768]{0:T(1024)S(1)} %add.463) | copy-start | bytes 9220
  200.0 29.3 %slice-start.5 = ((s8[4718592]{0:T(1024)(128)(4,1)}), s8[524288]{0:T(1024)(128)(4,1)S(1)}, s32[]{:S(2)}) async-start(s8[4718592]{0:T(1024)(128)(4,1)} %bitcast.256), calls=%async_computation.5 | async-start | bytes 1048576
  201.2 133.6 %copy-start.11 = (f32[512,768]{1,0:T(8,128)}, f32[512,768]{1,0:T(8,128)S(1)}, u32[]{:S(2)}) copy-start(f32[512,768]{1,0:T(8,128)S(1)} %get-tuple-element.354) | copy-start | bytes 4718596
  201.5 27.7 %slice-start.6 = ((s8[4718592]{0:T(1024)(128)(4,1)}), s8[4194304]{0:T(1024)(128)(4,1)S(1)}, s32[]{:S(2)}) async-start(s8[4718592]{0:T(1024)(128)(4,1)} %bitcast.256), calls=%async_computation.6 | async-start | bytes 8388608
  232.1 25.7 %copy-start.27 = (bf16[960,768]{1,0:T(8,128)(2,1)S(1)}, bf16[960,768]{1,0:T(8,128)(2,1)}, u32[]{:S(2)}) copy-start(bf16[960,768]{1,0:T(8,128)(2,1)} %get-tuple-element.535) | copy-start | bytes 4423684
  262.9 17.1 %copy-start.42 = (f32[2048]{0:T(1024)S(1)}, f32[2048]{0:T(1024)}, u32[]{:S(2)}) copy-start(f32[2048]{0:T(1024)} %convert_element_type.190) | copy-start | bytes 24580
  280.0 10.3 %copy-start.10 = (f32[2048,960]{0,1:T(8,128)S(1)}, f32[2048,960]{0,1:T(8,128)}, u32[]{:S(2)}) copy-start(f32[2048,960]{0,1:T(8,128)} %copy-done.9) | copy-start | bytes 23592964
  280.0 10.2 %copy-start.28 = (bf16[960,768]{1,0:T(8,128)(2,1)S(1)}, bf16[960,768]{1,0:T(8,128)(2,1)}, u32[]{:S(2)}) copy-start(bf16[960,768]{1,0:T(8,128)(2,1)} %get-tuple-element.535) | copy-start | bytes 4423684
  298.8 23.6 %copy-start.14 = (f32[512,768]{1,0:T(8,128)S(1)}, f32[512,768]{1,0:T(8,128)}, u32[]{:S(2)}) copy-start(f32[512,768]{1,0:T(8,128)} %copy-done.13) | copy-start | bytes 4718596
  324.8 10.0 %slice-start.3 = ((s8[4718592]{0:T(1024)(128)(4,1)}), s8[4194304]{0:T(1024)(128)(4,1)S(1)}, s32[]{:S(2)}) async-start(s8[4718592]{0:T(1024)(128)(4,1)} %bitcast.252), calls=%async_computation.3 | async-start | bytes 8388608
  359.7 18.4 %slice-start = ((s8[12582912]{0:T(1024)(128)(4,1)}), s8[4194304]{0:T(1024)(128)(4,1)S(1)}, s32[]{:S(2)}) async-start(s8[12582912]{0:T(1024)(128)(4,1)} %bitcast.194), calls=%async_computation | async-start | bytes 8388608
  359.7 18.4 %slice-start.1 = ((s8[12582912]{0:T(1024)(128)(4,1)}), s8[4194304]{0:T(1024)(128)(4,1)S(1)}, s32[]{:S(2)}) async-start(s8[12582912]{0:T(1024)(128)(4,1)} %bitcast.194), calls=%async_computation.1 | async-start | bytes 8388608
  415.0 109.1 %copy-start.46 = (s32[1024]{0:T(1024)S(1)}, s32[1024]{0:T(1024)}, u32[]{:S(2)}) copy-start(s32[1024]{0:T(1024)} %copy-done.45) | copy-start | bytes 12292
  415.0 109.1 %copy-start.58 = (f32[960,768]{1,0:T(8,128)S(1)}, f32[960,768]{1,0:T(8,128)}, u32[]{:S(2)}) copy-start(f32[960,768]{1,0:T(8,128)} %fusion.99) | copy-start | bytes 8847364
  528.9 27.4 %copy-start.40 = (f32[8,24]{1,0:T(8,128)S(1)}, f32[8,24]{1,0:T(8,128)}, u32[]{:S(2)}) copy-start(f32[8,24]{1,0:T(8,128)} %param.42) | copy-start | bytes 2308
  528.9 27.4 %copy-start.43 = (f32[8,24]{1,0:T(8,128)S(1)}, f32[8,24]{1,0:T(8,128)}, u32[]{:S(2)}) copy-start(f32[8,24]{1,0:T(8,128)} %param.50) | copy-start | bytes 2308
  528.9 27.4 %copy-start.44 = (f32[8,24]{1,0:T(8,128)S(1)}, f32[8,24]{1,0:T(8,128)}, u32[]{:S(2)}) copy-start(f32[8,24]{1,0:T(8,128)} %param.58) | copy-start | bytes 2308
  528.9 28.7 %copy-start.51 = (f32[96]{0:T(128)S(1)}, f32[96]{0:T(128)}, u32[]{:S(2)}) copy-start(f32[96]{0:T(128)} %param.43) | copy-start | bytes 1156
  528.9 28.7 %copy-start.52 = (f32[96]{0:T(128)S(1)}, f32[96]{0:T(128)}, u32[]{:S(2)}) copy-start(f32[96]{0:T(128)} %param.51) | copy-start | bytes 1156
  528.9 28.7 %copy-start.53 = (f32[96]{0:T(128)S(1)}, f32[96]{0:T(128)}, u32[]{:S(2)}) copy-start(f32[96]{0:T(128)} %param.59) | copy-start | bytes 1156
  528.9 30.6 %copy-start.34 = (f32[768,24]{0,1:T(8,128)S(1)}, f32[768,24]{0,1:T(8,128)}, u32[]{:S(2)}) copy-start(f32[768,24]{0,1:T(8,128)} %param.39) | copy-start | bytes 221188
  529.0 36.4 %copy-start.30 = (f32[96,768]{1,0:T(8,128)S(1)}, f32[96,768]{1,0:T(8,128)}, u32[]{:S(2)}) copy-start(f32[96,768]{1,0:T(8,128)} %param.41) | copy-start | bytes 884740
  (40 other events, 191.4 us)

commit v2 on v1

--- a/solution.py
+++ b/solution.py
@@ -198,17 +198,19 @@
     wires.sent()
 
 
-def ids_kernel(planes, x, out, send, recv, local):
+def ids_kernel(planes, x, small, out, small_out, send, recv, local):
     h, z, c = place()
     offsets = [(s, e) for s in range(planes) for e in range(2) if s or e]
     peers = [(h, 2 * lax.rem(z + s, planes) + lax.rem(c + e, 2)) for s, e in offsets]
-    greet(peers)
+    chips = [(across(h, q), 2 * lax.rem(z + s, planes) + c) for q in (1, 2, 3) for s in range(planes)]
+    greet(peers + chips)
     wires = Wires(send, recv)
-    mine = pltpu.make_async_copy(x, out.at[2 * z + c], local)
+    mine = pltpu.make_async_copy(x, out.at[2 * z + c], local.at[0])
     mine.start()
-    for to in peers:
-        wires.copy(x, out.at[2 * z + c], to)
-    for one in wires.made:
+    ids = [wires.copy(x, out.at[2 * z + c], to) for to in peers]
+    state = spread_start(wires, local.at[1], planes, lambda th, tz: small, small_out)
+    spread_finish(wires, planes, small_out, state)
+    for one in ids:
         one.wait_recv()
     mine.wait()
     wires.sent()
@@ -220,18 +222,6 @@
     greet(near(planes))
     wires = Wires(send, recv)
     gather_steps(wires, local, planes, list(zip(xs, outs)))
-    wires.sent()
-
-
-def fetch_kernel(planes, count, *refs):
-    parcels, xs = refs[0], refs[1 : 1 + count]
-    out, outs = refs[1 + count], refs[2 + count : 2 + 2 * count]
-    send, recv, local = refs[2 + 2 * count :]
-    greet(every_chip(planes))
-    wires = Wires(send, recv)
-    state = spread_start(wires, local.at[count], planes, lambda h, z: parcels.at[h, z], out)
-    gather_steps(wires, local, planes, list(zip(xs, outs)))
-    spread_finish(wires, planes, out, state)
     wires.sent()
 
 
@@ -391,6 +381,380 @@
     wires.sent()
 
 
+def guarded(ok, act):
+    if ok is None:
+        act()
+    else:
+        pl.when(ok)(act)
+
+
+class Lines:
+    def __init__(self, send, recv):
+        self.send, self.recv, self.used, self.made = send, recv, 0, []
+
+    def make(self, src, dst, to, ok):
+        i = self.used
+        self.used += 1
+        one = pltpu.make_async_remote_copy(
+            src_ref=src,
+            dst_ref=dst,
+            send_sem=self.send.at[i],
+            recv_sem=self.recv.at[i],
+            device_id=to,
+            device_id_type=MESH,
+        )
+        self.made.append((one, ok))
+        return one
+
+    def sent(self):
+        for one, ok in self.made:
+            guarded(ok, one.wait_send)
+
+
+def line_steps(planes):
+    return [0] + [d * s for s in range(1, planes) for d in (1, -1)]
+
+
+class Gather:
+    def __init__(self, wires, local, planes, pairs):
+        self.wires, self.planes, self.pairs = wires, planes, pairs
+        h, z, c = place()
+        self.h, self.z, self.c = h, z, c
+        row = 2 * z + c
+        self.sib = (h, 2 * z + 1 - c)
+        self.hx, self.hy, self.hd = across(h, 1), across(h, 2), across(h, 3)
+        self.xn, self.yn = (self.hx, row), (self.hy, row)
+        self.at, self.have, self.on = {0: z}, {0: None}, {}
+        for s in line_steps(planes)[1:]:
+            t = z - s
+            self.have[s] = (t >= 0) & (t < planes)
+            self.at[s] = jnp.clip(t, 0, planes - 1)
+        for s in range(planes - 1):
+            for d in (1, -1):
+                u = z + d
+                ok = (u >= 0) & (u < planes)
+                self.on[d, s] = (ok & self.have[d * s]) if s else ok
+        self.here = []
+        for k, (x, out) in enumerate(pairs):
+            one = pltpu.make_async_copy(x, out.at[h, z, c], local.at[k])
+            one.start()
+            self.here.append(one)
+        self.line, self.copies = {}, {}
+
+    def onward(self, k, d, s):
+        x, out = self.pairs[k]
+        t = self.at[d * s]
+        ref = x if s == 0 else out.at[self.h, t, self.c]
+        u = jnp.clip(self.z + d, 0, self.planes - 1)
+        ok = self.on[d, s]
+        one = self.wires.make(ref, out.at[self.h, t, self.c], (self.h, 2 * u + self.c), ok)
+        self.line[k, d, s] = one
+        guarded(ok, one.start)
+
+    def launch(self, k, s):
+        x, out = self.pairs[k]
+        t, ok = self.at[s], self.have[s]
+        here = out.at[self.h, t, self.c]
+        ref = x if s == 0 else here
+        if s == 0:
+            self.onward(k, 1, 0)
+            self.onward(k, -1, 0)
+        else:
+            d, a = (1, s) if s > 0 else (-1, -s)
+            guarded(ok, self.line[k, d, a - 1].wait_recv)
+            if a < self.planes - 1:
+                self.onward(k, d, a)
+        make = self.wires.make
+        ones = [make(ref, here, to, ok) for to in (self.xn, self.yn, self.sib)]
+        self.copies[k, s, "x"], self.copies[k, s, "y"], self.copies[k, s, "s"] = ones
+
+        def act():
+            for one in ones:
+                one.start()
+
+        guarded(ok, act)
+
+    def relay(self, k, s):
+        out = self.pairs[k][1]
+        t, ok = self.at[s], self.have[s]
+        first, second = split(out.shape[3])
+        make, got = self.wires.make, self.copies
+        gx, gy = out.at[self.hx, t, self.c], out.at[self.hy, t, self.c]
+        got[k, s, "yd"] = make(gx.at[second], gx.at[second], self.yn, ok)
+        got[k, s, "sx"] = make(gx, gx, self.sib, ok)
+        got[k, s, "xd"] = make(gy.at[first], gy.at[first], self.xn, ok)
+        got[k, s, "sy"] = make(gy, gy, self.sib, ok)
+
+        def act():
+            got[k, s, "x"].wait_recv()
+            got[k, s, "yd"].start()
+            got[k, s, "sx"].start()
+            got[k, s, "y"].wait_recv()
+            got[k, s, "xd"].start()
+            got[k, s, "sy"].start()
+
+        guarded(ok, act)
+
+    def finish(self, k, s):
+        out = self.pairs[k][1]
+        t, ok = self.at[s], self.have[s]
+        got = self.copies
+        gd = out.at[self.hd, t, self.c]
+        got[k, s, "sd"] = self.wires.make(gd, gd, self.sib, ok)
+
+        def act():
+            got[k, s, "yd"].wait_recv()
+            got[k, s, "xd"].wait_recv()
+            got[k, s, "sd"].start()
+
+        guarded(ok, act)
+
+    def done(self, k, s):
+        if s == 0:
+            self.here[k].wait()
+
+        def act():
+            for part in ("s", "sx", "sy", "sd"):
+                self.copies[k, s, part].wait_recv()
+
+        guarded(self.have[s], act)
+
+
+def line_wires(planes, count):
+    return count * (2 * planes - 1) * 9
+
+
+def mul(left, right, left_dim=1, right_dim=0):
+    return lax.dot_general(
+        left, right, (((left_dim,), (right_dim,)), ((), ())), preferred_element_type=jnp.float32
+    )
+
+
+def unit_of(values):
+    center = values - jnp.mean(values, axis=-1, keepdims=True)
+    scale = lax.rsqrt(jnp.mean(center * center, axis=-1, keepdims=True) + EPSILON)
+    return center * scale, scale
+
+
+ERF_TOP = (
+    -2.72614225801306e-10,
+    2.77068142495902e-08,
+    -2.10102402082508e-06,
+    -5.69250639462346e-05,
+    -7.34990630326855e-04,
+    -2.95459980854025e-03,
+    -1.60960333262415e-02,
+)
+ERF_LOW = (
+    -1.45660718464996e-05,
+    -2.13374055278905e-04,
+    -1.68282697438203e-03,
+    -7.37332916720468e-03,
+    -1.42647390514189e-02,
+)
+
+
+def erf(x):
+    x = jnp.clip(x, -4.0, 4.0)
+    square = x * x
+    top = jnp.full_like(x, ERF_TOP[0])
+    for c in ERF_TOP[1:]:
+        top = top * square + c
+    bottom = jnp.full_like(x, ERF_LOW[0])
+    for c in ERF_LOW[1:]:
+        bottom = bottom * square + c
+    return x * top / bottom
+
+
+def gelu_parts(u, ramp):
+    cdf = 0.5 + 0.5 * erf(u * (0.5**0.5))
+    density = jnp.exp(-0.5 * u * u) * 0.3989422804014327
+    return u * cdf * ramp, (cdf + u * density) * ramp
+
+
+def head_slice(ref, head, part):
+    group, i = head // 3, head % 3
+    start = (3 * i + part) * HD
+    return ref[group, :, start : start + HD]
+
+
+def masked_scores(q, k, labels_col, labels_row):
+    s = mul(q, k, 1, 1) * HD**-0.5
+    return jnp.where(labels_col == labels_row, s, -1000000000.0)
+
+
+def forward_kernel(planes, room, *refs):
+    (parcels, misc, wq, wu, wd, home, extra, lab_col, lab_row, norms, bias, ramp, chosen) = refs[:13]
+    (misc_all, wq_all, wu_all, wd_all) = refs[13:17]
+    (unit0, scale0, mixed, lse, heads, unit1, scale1, active, slope, unit2, scale2, picked) = refs[
+        17:29
+    ]
+    (box, misc_v, wq_v, wu_v, wd_v, hidden, total) = refs[29:36]
+    send, recv, local, send2, recv2, loads = refs[36:]
+    low = jnp.bfloat16
+    h, z, c = place()
+    greet(every_chip(planes))
+    lines = Lines(send, recv)
+    posts = Wires(send2, recv2)
+    pairs = [(misc, misc_all), (wq, wq_all), (wu, wu_all), (wd, wd_all)]
+    gather = Gather(lines, local, planes, pairs)
+    tokens, width = unit0.shape
+    state = {}
+
+    def post():
+        state["post"] = spread_start(posts, local.at[4], planes, lambda th, tz: parcels.at[th, tz], box)
+
+    def opened():
+        spread_finish(posts, planes, box, state["post"])
+
+    def load(k, view):
+        ones = []
+        for t in range(planes):
+            one = pltpu.make_async_copy(
+                pairs[k][1].at[:, t], view.at[:, t], loads.at[k * planes + t]
+            )
+            one.start()
+            ones.append(one)
+        return ones
+
+    def wait(ones):
+        for one in ones:
+            one.wait()
+
+    def start_norm():
+        wait(load(0, misc_v))
+        spots = lax.broadcasted_iota(jnp.int32, (tokens, box.shape[3] * 8 * planes), 1)
+        marks = (home[...] == spots).astype(jnp.float32).astype(low)
+        rows = box[...].reshape(-1, width)
+        looked = mul(marks, rows) + extra[...]
+        pieces = misc_v[...].astype(jnp.float32)
+        share = misc_v.shape[3] // 2
+        places = pieces[:, :, :, share:, :SEQ].reshape(width, SEQ).T
+        unit, scale = unit_of(looked + places)
+        unit0[...] = unit
+        scale0[...] = scale
+        hidden[...] = unit * norms[0:1, :] + norms[1:2, :]
+
+    def project(group):
+        weight = wq_v[group].reshape(width, wq_v.shape[4])
+        mixed[group] = mul(hidden[...].astype(low), weight).astype(low)
+
+    def attend(pair):
+        outs = []
+        for head in (2 * pair, 2 * pair + 1):
+            q, k, v = (head_slice(mixed, head, j) for j in range(3))
+            s = masked_scores(q, k, lab_col[...], lab_row[...])
+            top = jnp.max(s, axis=1, keepdims=True)
+            e = jnp.exp(s - top)
+            sums = jnp.sum(e, axis=1, keepdims=True)
+            lse[:, head : head + 1] = top + jnp.log(sums)
+            p = (e / sums).astype(low)
+            scale = 1.0 if head < OLD_HEADS else STEP / RAMP
+            outs.append((mul(p, v) * scale).astype(low))
+        heads[:, 2 * HD * pair : 2 * HD * (pair + 1)] = jnp.concatenate(outs, axis=1)
+
+    def middle():
+        share = misc_v.shape[3] // 2
+        weight = misc_v[...].astype(jnp.float32)[:, :, :, :share].reshape(width, width).astype(low)
+        value = hidden[...] + mul(heads[...], weight, 1, 1) + norms[6:7, :]
+        unit, scale = unit_of(value)
+        unit1[...] = unit
+        scale1[...] = scale
+        hidden[...] = unit * norms[2:3, :] + norms[3:4, :]
+        total[...] = hidden[...] + norms[7:8, :]
+
+    def chunk(t):
+        one = pltpu.make_async_copy(wu_all.at[:, t], wu_v.at[0], loads.at[2 * planes])
+        two = pltpu.make_async_copy(wd_all.at[:, t], wd_v.at[0], loads.at[2 * planes + 1])
+        one.start()
+        two.start()
+        one.wait()
+        units = wu_v.shape[1] * 2 * wu_v.shape[3]
+        u = mul(hidden[...].astype(low), wu_v[0].reshape(units, width), 1, 1) + bias[t]
+        value, rise = gelu_parts(u, ramp[t])
+        value = value.astype(low)
+        active[t] = value
+        slope[t] = rise.astype(low)
+        two.wait()
+        total[...] += mul(value, wd_v[0].reshape(units, width))
+
+    def last():
+        unit, scale = unit_of(total[...])
+        unit2[...] = unit
+        scale2[...] = scale
+        final = (unit * norms[4:5, :] + norms[5:6, :]).astype(low)
+        spots = lax.broadcasted_iota(jnp.int32, (chosen.shape[0], tokens), 1)
+        marks = (chosen[...] == spots).astype(jnp.float32).astype(low)
+        picked[...] = mul(marks, final).astype(low)
+
+    near_first = []
+    for j in range(planes):
+        spot = jnp.int32(0)
+        for zz in range(planes):
+            ranked = sorted(range(planes), key=lambda t: (abs(t - zz), t))
+            spot = jnp.where(z == zz, ranked[j], spot)
+        near_first.append(spot)
+
+    lag = 3
+    steps = line_steps(planes)
+    far = [s for s in steps if abs(s) > 1]
+    early = [(k, s) for k in range(2) for s in (0,)]
+    early += [(k, s) for k in range(2) for s in (1, -1)] + [(k, s) for k in range(2) for s in far]
+    whole = early + [(k, 0) for k in (2, 3)]
+    whole += [(k, s) for a in range(1, planes) for k in (2, 3) for s in (a, -a)]
+    events = []
+    for i in range(len(whole) + 2 * lag):
+        if i < len(whole):
+            events.append((gather.launch, *whole[i]))
+        if lag <= i < len(whole) + lag:
+            events.append((gather.relay, *whole[i - lag]))
+        if i >= 2 * lag:
+            events.append((gather.finish, *whole[i - 2 * lag]))
+    position = events.index((gather.launch, *whole[6]))
+    ready = events.index((gather.finish, *early[-1])) + 1
+    for event, k, s in events[:position]:
+        event(k, s)
+    post()
+    for event, k, s in events[position:ready]:
+        event(k, s)
+    opened()
+    for s in steps:
+        gather.done(0, s)
+    rest = events[ready:]
+    later = rest.index((gather.finish, 3, -2)) + 1 if planes > 2 else len(rest)
+
+    def settle():
+        for s in steps:
+            gather.done(1, s)
+        wait(load(1, wq_v))
+
+    def settle_far(a):
+        for k in (2, 3):
+            for s in (a, -a) if a else (0,):
+                gather.done(k, s)
+
+    work = [start_norm, lambda: (settle(), project(0))]
+    work += [functools.partial(project, g) for g in range(1, 4)]
+    work += [functools.partial(attend, p) for p in range(6)]
+    work.append(middle)
+    work.append(lambda: (settle_far(0), chunk(near_first[0])))
+    work.append(lambda: (settle_far(1), chunk(near_first[1])))
+    count = len(work)
+    for i, act in enumerate(work):
+        act()
+        for event, k, s in rest[later * i // count : later * (i + 1) // count]:
+            event(k, s)
+    for a in range(2, planes):
+        settle_far(a)
+        chunk(near_first[a])
+        if a == 2:
+            for event, k, s in rest[later:]:
+                event(k, s)
+    last()
+    posts.sent()
+    lines.sent()
+
+
 def params(number):
     return pltpu.CompilerParams(
         collective_id=number, has_side_effects=True, vmem_limit_bytes=56 << 20
@@ -427,33 +791,80 @@
     def __init__(self, planes):
         self.planes = planes
 
-    def ids(self, block):
+    def ids(self, block, small):
         planes = self.planes
-        wires = 2 * planes - 1
+        wires = 2 * planes - 1 + spread_wires(planes)
         return pl.pallas_call(
             functools.partial(ids_kernel, planes),
-            out_shape=jax.ShapeDtypeStruct((2 * planes, *block.shape), block.dtype),
-            in_specs=[ANY],
-            out_specs=ANY,
-            scratch_shapes=[dma(wires), dma(wires), pltpu.SemaphoreType.DMA],
+            out_shape=[
+                jax.ShapeDtypeStruct((2 * planes, *block.shape), block.dtype),
+                jax.ShapeDtypeStruct((2, 4, planes, *small.shape), small.dtype),
+            ],
+            in_specs=[VMEM] * 2,
+            out_specs=[VMEM] * 2,
+            scratch_shapes=[dma(wires), dma(wires), dma(2)],
             compiler_params=params(1),
             name="ids",
-        )(block)
-
-    def fetch(self, parcels, blocks):
-        planes, count = self.planes, len(blocks)
-        wires = gather_wires(planes, count) + spread_wires(planes)
+        )(block, small)
+
+    def forward(self, parcels, blocks, home, extra, labels, norms, bias, ramp, chosen):
+        planes = self.planes
+        low, f32 = jnp.bfloat16, jnp.float32
+        tokens, width = extra.shape
+        units = bias.shape[2]
+        gathered = [jax.ShapeDtypeStruct((4, planes, 2, *b.shape), b.dtype) for b in blocks]
+        saved = [
+            ((tokens, width), f32),
+            ((tokens, 1), f32),
+            ((4, tokens, blocks[1].shape[1]), low),
+            ((tokens, 128), f32),
+            ((tokens, width), low),
+            ((tokens, width), f32),
+            ((tokens, 1), f32),
+            ((planes, tokens, units), low),
+            ((planes, tokens, units), low),
+            ((tokens, width), f32),
+            ((tokens, 1), f32),
+            ((chosen.shape[0], width), low),
+        ]
+        count = line_wires(planes, 4)
+        spread = spread_wires(planes)
+        share = blocks[2].shape[0]
         result = pl.pallas_call(
-            functools.partial(fetch_kernel, planes, count),
-            out_shape=[jax.ShapeDtypeStruct((2, *parcels.shape), parcels.dtype)]
-            + [jax.ShapeDtypeStruct((4, planes, 2, *b.shape), b.dtype) for b in blocks],
-            in_specs=[ANY] * (1 + count),
-            out_specs=[ANY] * (1 + count),
-            scratch_shapes=[dma(wires), dma(wires), dma(count + 1)],
+            functools.partial(forward_kernel, planes, ROOM),
+            out_shape=gathered + [jax.ShapeDtypeStruct(s, t) for s, t in saved],
+            in_specs=[ANY] * 5 + [VMEM] * 8,
+            out_specs=[ANY] * 4 + [VMEM] * len(saved),
+            scratch_shapes=[
+                pltpu.VMEM((2, *parcels.shape), low),
+                pltpu.VMEM(gathered[0].shape, low),
+                pltpu.VMEM(gathered[1].shape, low),
+                pltpu.VMEM((1, 4, 2, share, width), low),
+                pltpu.VMEM((1, 4, 2, share, width), low),
+                pltpu.VMEM((tokens, width), f32),
+                pltpu.VMEM((tokens, width), f32),
+                dma(count),
+                dma(count),
+                dma(5),
+                dma(spread),
+                dma(spread),
+                dma(2 * planes + 2),
+            ],
             compiler_params=params(2),
-            name="fetch",
-        )(parcels, *blocks)
-        return result[0], result[1:]
+            name="forward",
+        )(
+            parcels,
+            *blocks,
+            home,
+            extra,
+            labels.reshape(-1, 1),
+            labels.reshape(1, -1),
+            norms,
+            bias,
+            ramp,
+            chosen.reshape(-1, 1),
+        )
+        return result[:4], result[4:]
 
     def deliver(self, parcels):
         planes = self.planes
@@ -548,15 +959,19 @@
     def __init__(self, planes):
         self.planes = planes
 
-    def ids(self, block):
-        return lax.all_gather(block, "row")
+    def ids(self, block, small):
+        return lax.all_gather(block, "row"), self.small(small, 0)
 
     def gather(self, block):
         whole = lax.all_gather(block, ("head", "row"))
         return whole.reshape(4, self.planes, 2, *block.shape)
 
-    def fetch(self, parcels, blocks):
-        return self.deliver(parcels), [self.gather(b) for b in blocks]
+    def forward(self, parcels, blocks, home, extra, labels, norms, bias, ramp, chosen):
+        parcels = self.deliver(parcels)
+        gathered = [self.gather(b) for b in blocks]
+        return gathered, forward_plain(
+            parcels, gathered, home, extra, labels, norms, bias, ramp, chosen
+        )
 
     def deliver(self, parcels):
         shape = parcels.shape
@@ -592,14 +1007,7 @@
     )
 
 
-def normalize(values, gain, shift):
-    center = values - jnp.mean(values, axis=-1, keepdims=True)
-    scale = lax.rsqrt(jnp.mean(center * center, axis=-1, keepdims=True) + EPSILON)
-    unit = center * scale
-    return (unit * gain + shift, unit, scale)
-
-
-def normalize_back(grad, unit, scale, gain):
+def unit_back(grad, unit, scale, gain):
     inner = grad * gain
     back = scale * (
         inner
@@ -607,6 +1015,57 @@
         - unit * jnp.mean(inner * unit, axis=-1, keepdims=True)
     )
     return (back, grad * unit)
+
+
+def by_plane(blocks):
+    planes, lanes = blocks.shape[1], blocks.shape[4]
+    return blocks.transpose(1, 0, 2, 3, 4).reshape(planes, -1, lanes)
+
+
+def heads_of(mixed):
+    tokens = mixed.shape[1]
+    parts = mixed.reshape(4, tokens, -1, 3, HD).transpose(3, 1, 0, 2, 4)
+    parts = parts.reshape(3, tokens, -1, HD)
+    return parts[0], parts[1], parts[2]
+
+
+def forward_plain(parcels, gathered, home, extra, labels, norms, bias, ramp, chosen):
+    low = jnp.bfloat16
+    misc, wq, wu, wd = gathered
+    tokens, width = extra.shape
+    share = misc.shape[3] // 2
+    rows = parcels.reshape(-1, width)
+    looked = jnp.dot(
+        (home == jnp.arange(rows.shape[0])[None, :]).astype(low),
+        rows,
+        preferred_element_type=jnp.float32,
+    )
+    places = misc[:, :, :, share:, :SEQ].reshape(width, SEQ).T.astype(jnp.float32)
+    unit0, scale0 = unit_of(looked + extra + places)
+    normed = unit0 * norms[0] + norms[1]
+    weight = wq.reshape(4, width, wq.shape[4])
+    mixed = jnp.einsum("td,hdj->htj", normed.astype(low), weight, preferred_element_type=jnp.float32)
+    mixed = mixed.astype(low)
+    query, keys, values = heads_of(mixed)
+    attended, summary = attend_fwd(query, keys, values, labels)
+    head_ramp = jnp.where(jnp.arange(query.shape[1]) < OLD_HEADS, 1.0, STEP / RAMP)
+    heads = (attended * head_ramp[:, None]).astype(low).reshape(tokens, width)
+    lse = jnp.pad(summary.T, ((0, 0), (0, 128 - summary.shape[0])))
+    weight = misc[:, :, :, :share].reshape(width, width)
+    unit1, scale1 = unit_of(normed + contract(heads, weight, 1, 1) + norms[6])
+    hidden = unit1 * norms[2] + norms[3]
+    u = jnp.einsum(
+        "td,pud->ptu", hidden.astype(low), by_plane(wu), preferred_element_type=jnp.float32
+    )
+    value, rise = gelu_parts(u + bias, ramp)
+    active = value.astype(low)
+    down = jnp.einsum("ptu,pud->td", active, by_plane(wd), preferred_element_type=jnp.float32)
+    unit2, scale2 = unit_of(hidden + down + norms[7])
+    final = (unit2 * norms[4] + norms[5]).astype(low)
+    marks = (chosen[:, None] == jnp.arange(tokens)[None, :]).astype(low)
+    picked = jnp.dot(marks, final, preferred_element_type=jnp.float32).astype(low)
+    slope = rise.astype(low)
+    return (unit0, scale0, mixed, lse, heads, unit1, scale1, active, slope, unit2, scale2, picked)
 
 
 def score_block(query, keys, labels):
@@ -701,14 +1160,28 @@
     tokens = token_ids.shape[0] // HEADS
     inner = up_weight.shape[1] * devices
 
+    share = width // devices
+    share_inner = inner // devices
+
     labels_all = segment_ids.reshape(HEADS, tokens)
     slots = masked_pos.shape[1] // HEADS
     live = labels_at(segment_ids, masked_pos[0])
     target = jnp.where(live, masked_target[0], -1)
+    small = jnp.concatenate([norm_params.reshape(-1), up_bias]).astype(low)
+    small_rows = -(-small.shape[0] // 2048) * 16
     words = token_ids.shape[0] + target.shape[0]
     lines = -(-words // 1024) * 8
-    numbers = wire.ids(padded(jnp.concatenate([token_ids, target]), lines, 128))
+    numbers, small_all = wire.ids(
+        padded(jnp.concatenate([token_ids, target]), lines, 128), padded(small, small_rows, 128)
+    )
     numbers = numbers.reshape(row_count, lines * 128)
+    small_all = jnp.moveaxis(small_all.reshape(2, HEADS, planes, -1), 0, 2).astype(jnp.float32)
+    norms = small_all[..., : 8 * share].reshape(devices, 8, share)
+    norms = norms.transpose(1, 0, 2).reshape(8, width)
+    bias = small_all[..., 8 * share : 8 * share + share_inner]
+    bias = bias.transpose(1, 0, 2, 3).reshape(planes, 1, -1)
+    ramp = jnp.where(jnp.arange(inner) < OLD_FF, 1.0, STEP / RAMP).astype(jnp.float32)
+    ramp = ramp.reshape(HEADS, planes, -1).transpose(1, 0, 2).reshape(planes, 1, -1)
     ids = numbers[:, : token_ids.shape[0]].reshape(planes, 2, HEADS, tokens)
     ids = ids.transpose(2, 0, 1, 3).reshape(HEADS * planes, 2 * tokens)
     targets = numbers[:, token_ids.shape[0] : words].reshape(row_count, HEADS, slots)
@@ -740,10 +1213,12 @@
         marks = which.reshape(-1)[:, None] == jnp.arange(vocab_part)[None, :]
         return marks.astype(low)
 
+    def seats(turn):
+        seat = own_rank - turn * ROOM
+        return jnp.where((seat >= 0) & (seat < ROOM), own_home * ROOM + seat, -1)[:, None]
+
     def token_marks(turn):
-        seat = own_rank - turn * ROOM
-        seat = jnp.where((seat >= 0) & (seat < ROOM), own_home * ROOM + seat, -1)
-        return (seat[:, None] == jnp.arange(devices * ROOM)[None, :]).astype(low)
+        return (seats(turn) == jnp.arange(devices * ROOM)[None, :]).astype(low)
 
     def parcels_of(turn):
         picked = jnp.dot(parcel_marks(turn), table, preferred_element_type=jnp.float32)
@@ -756,74 +1231,46 @@
             preferred_element_type=jnp.float32,
         )
 
-    share = width // devices
-    share_inner = inner // devices
-    misc = jnp.concatenate(
-        [
-            out_weight.T.reshape(-1),
-            position_table.T.reshape(-1),
-            norm_params.reshape(-1),
-            up_bias,
-        ]
-    ).astype(low)
-    misc_rows = -(-misc.shape[0] // (16 * width)) * 16
-    parcels, gathered = wire.fetch(
-        parcels_of(0),
-        [
-            padded(misc, misc_rows, width),
-            qkv_weight.astype(low),
-            up_weight.T.astype(low),
-            down_weight.astype(low),
-        ],
-    )
-    looked = opened(parcels, 0)
-
     def again(state):
         turn, so_far = state
         return turn + 1, so_far + opened(wire.deliver(parcels_of(turn)), turn)
 
-    _, looked = lax.while_loop(lambda state: state[0] < rounds, again, (jnp.int32(1), looked))
-
-    misc_all = gathered[0].reshape(devices, misc_rows * width)
+    _, extra = lax.while_loop(
+        lambda state: state[0] < rounds,
+        again,
+        (jnp.int32(1), jnp.zeros((tokens, width), jnp.float32)),
+    )
+
+    labels = lax.dynamic_index_in_dim(labels_all, head, 0, keepdims=False)
+    chosen = lax.dynamic_slice_in_dim(masked_pos[0], head * slots, slots, 0) - head * tokens
+    misc = jnp.concatenate(
+        [out_weight.T, jnp.pad(position_table.T, ((0, 0), (0, width - SEQ)))], axis=0
+    )
+    gathered, saved = wire.forward(
+        parcels_of(0),
+        [misc.astype(low), qkv_weight.astype(low), up_weight.T.astype(low), down_weight.astype(low)],
+        seats(0),
+        extra,
+        labels,
+        norms,
+        bias,
+        ramp,
+        chosen,
+    )
+    unit_zero, scale_zero, mixed, lse, heads_low, unit_one, scale_one = saved[:7]
+    active, slope, unit_two, scale_two, picked = saved[7:]
+    out_full = gathered[0][:, :, :, :share].reshape(width, width)
     qkv_full = gathered[1].reshape(HEADS, width, qkv_weight.shape[1])
-    up_full = gathered[2].reshape(inner, width)
-    down_full = gathered[3].reshape(inner, width)
-    cuts = [share * width, share * SEQ, share * 8, share_inner]
-    starts = [sum(cuts[:i]) for i in range(5)]
-    pieces = [misc_all[:, starts[i] : starts[i + 1]] for i in range(4)]
-    out_full = pieces[0].reshape(width, width)
-    places = pieces[1].reshape(width, SEQ).T
-    norms = pieces[2].reshape(devices, 8, share).transpose(1, 0, 2).reshape(8, width)
-    norms = norms.astype(jnp.float32)
-    bias = pieces[3].reshape(inner).astype(jnp.float32)
-
-    labels = lax.dynamic_index_in_dim(labels_all, head, 0, keepdims=False)
-    start_sum = looked + places.astype(jnp.float32)
-    normed, unit_zero, scale_zero = normalize(start_sum, norms[0], norms[1])
-    normed_low = normed.astype(low)
-    mixed = jnp.einsum("td,hdj->thj", normed_low, qkv_full, preferred_element_type=jnp.float32)
-    mixed = mixed.astype(low).reshape(tokens, -1, 3, HD)
-    heads = mixed.shape[1]
-    query, keys, values = (mixed[:, :, 0], mixed[:, :, 1], mixed[:, :, 2])
-    attended, summary = attend_fwd(query, keys, values, labels)
+    up_full, down_full = by_plane(gathered[2]), by_plane(gathered[3])
+    normed_low = (unit_zero * norms[0] + norms[1]).astype(low)
+    hidden_low = (unit_one * norms[2] + norms[3]).astype(low)
+    query, keys, values = heads_of(mixed)
+    heads = query.shape[1]
+    summary = lse[:, :heads].T
     head_ramp = jnp.where(jnp.arange(heads) < OLD_HEADS, 1.0, STEP / RAMP).astype(jnp.float32)
-    heads_low = (attended * head_ramp[:, None]).astype(low).reshape(tokens, heads * HD)
-    projected = contract(heads_low, out_full, 1, 1)
-    hidden, unit_one, scale_one = normalize(normed + projected + norms[6], norms[2], norms[3])
-    hidden_low = hidden.astype(low)
-    upper = contract(hidden_low, up_full, 1, 1) + bias
-    neuron_ramp = jnp.where(jnp.arange(inner) < OLD_FF, 1.0, STEP / RAMP).astype(jnp.float32)
-    activated, gelu_pull = jax.vjp(
-        lambda u: jax.nn.gelu(u, approximate=False) * neuron_ramp, upper
-    )
-    active_low = activated.astype(low)
-    lowered = jnp.dot(active_low, down_full, preferred_element_type=jnp.float32) + norms[7]
-    final, unit_two, scale_two = normalize(hidden + lowered, norms[4], norms[5])
-
-    chosen = lax.dynamic_slice_in_dim(masked_pos[0], head * slots, slots, 0) - head * tokens
+
     chosen_marks = chosen[:, None] == jnp.arange(tokens)[None, :]
-    picked = jnp.dot(chosen_marks.astype(low), final.astype(low), preferred_element_type=jnp.float32)
-    all_rows = wire.rows(picked.astype(low)).reshape(devices * slots, width)
+    all_rows = wire.rows(picked).reshape(devices * slots, width)
     valid = (targets >= 0).astype(jnp.float32)
     logits = contract(all_rows, table, 1, 1)
     hits = jnp.arange(vocab_part)[None, :] == (targets - device * vocab_part)[:, None]
@@ -850,14 +1297,18 @@
         (((0,), (0,)), ((), ())),
         precision=lax.Precision.HIGHEST,
     )
-    grad_sum, gain_two = normalize_back(grad_final, unit_two, scale_two, norms[4])
+    grad_sum, gain_two = unit_back(grad_final, unit_two, scale_two, norms[4])
     grad_sum_low = grad_sum.astype(low)
-    grad_down = contract(active_low, grad_sum_low, 0, 0)
-    grad_upper = gelu_pull(contract(grad_sum_low, down_full, 1, 1))[0]
+    f32 = jnp.float32
+    grad_down = jnp.einsum("ptu,td->pud", active, grad_sum_low, preferred_element_type=f32)
+    grad_upper = jnp.einsum("td,pud->ptu", grad_sum_low, down_full, preferred_element_type=f32)
+    grad_upper = grad_upper * slope.astype(f32)
     grad_upper_low = grad_upper.astype(low)
-    grad_up = contract(grad_upper_low, hidden_low, 0, 0)
-    grad_hidden = grad_sum + jnp.dot(grad_upper_low, up_full, preferred_element_type=jnp.float32)
-    grad_res, gain_one = normalize_back(grad_hidden, unit_one, scale_one, norms[2])
+    grad_up = jnp.einsum("ptu,td->pud", grad_upper_low, hidden_low, preferred_element_type=f32)
+    grad_hidden = grad_sum + jnp.einsum(
+        "ptu,pud->td", grad_upper_low, up_full, preferred_element_type=f32
+    )
+    grad_res, gain_one = unit_back(grad_hidden, unit_one, scale_one, norms[2])
     grad_res_low = grad_res.astype(low)
     grad_out = contract(grad_res_low, heads_low, 0, 0)
     grad_heads = jnp.dot(grad_res_low, out_full, preferred_element_type=jnp.float32).astype(low)
@@ -872,7 +1323,7 @@
     grad_normed = grad_res + jnp.einsum(
         "thj,hdj->td", grad_mixed_low, qkv_full, preferred_element_type=jnp.float32
     )
-    grad_start, gain_zero = normalize_back(grad_normed, unit_zero, scale_zero, norms[0])
+    grad_start, gain_zero = unit_back(grad_normed, unit_zero, scale_zero, norms[0])
     grad_start_low = grad_start.astype(low)
     grad_norms = jnp.stack(
         [
@@ -886,7 +1337,11 @@
             jnp.sum(grad_sum, axis=0),
         ]
     )
-    grad_bias = jnp.sum(grad_upper, axis=0)
+    grad_bias = jnp.sum(grad_upper, axis=1).reshape(planes, HEADS, 2 * share_inner)
+
+    def by_head(grad):
+        grad = grad.reshape(planes, HEADS, 2, share_inner, width).astype(low)
+        return grad.transpose(1, 0, 2, 3, 4)
 
     def parcels_back(turn):
         back = contract(token_marks(turn), grad_start_low, 0, 0).astype(low)
@@ -895,23 +1350,32 @@
     def unpacked(parcels, turn):
         return contract(parcel_marks(turn), parcels.reshape(-1, width), 0, 0)
 
+    flat = jnp.concatenate(
+        [
+            grad_norms.reshape(8, devices, share).transpose(1, 0, 2).reshape(devices, -1),
+            grad_bias.transpose(1, 0, 2).reshape(devices, -1),
+        ],
+        axis=1,
+    )
+    more_rows = -(-flat.shape[1] // width)
+    misc_rows = -(-(2 * share + more_rows) // 16) * 16
+    flat = jnp.pad(flat, ((0, 0), (0, more_rows * width - flat.shape[1])))
     grad_misc = jnp.concatenate(
         [
-            grad_out.reshape(devices, -1),
-            grad_start.T.reshape(devices, -1),
-            grad_norms.reshape(8, devices, share).transpose(1, 0, 2).reshape(devices, -1),
-            grad_bias.reshape(devices, -1),
+            grad_out.reshape(devices, share, width),
+            jnp.pad(grad_start.T, ((0, 0), (0, width - SEQ))).reshape(devices, share, width),
+            flat.reshape(devices, more_rows, width),
+            jnp.zeros((devices, misc_rows - more_rows - 2 * share, width), jnp.float32),
         ],
         axis=1,
     ).astype(low)
-    grad_misc = jnp.pad(grad_misc, ((0, 0), (0, misc_rows * width - grad_misc.shape[1])))
     parcels, summed = wire.give(
         parcels_back(0),
         [
             grad_misc.reshape(HEADS, planes, 2, misc_rows, width),
             grad_qkv.astype(low).reshape(HEADS, planes, 2, *qkv_weight.shape),
-            grad_up.astype(low).reshape(HEADS, planes, 2, share_inner, width),
-            grad_down.astype(low).reshape(HEADS, planes, 2, share_inner, width),
+            by_head(grad_up),
+            by_head(grad_down),
         ],
     )
     grad_table = grad_table + unpacked(parcels, 0)
@@ -923,16 +1387,16 @@
     _, grad_table = lax.while_loop(
         lambda state: state[0] < rounds, again_back, (jnp.int32(1), grad_table)
     )
-    misc_sum = summed[0].reshape(-1)
+    flat = summed[0][2 * share : 2 * share + more_rows].reshape(-1)
     grads = (
         grad_table,
-        misc_sum[starts[1] : starts[2]].reshape(share, SEQ).T,
+        summed[0][share : 2 * share, :SEQ].T,
         summed[1],
-        misc_sum[starts[0] : starts[1]].reshape(share, width).T,
+        summed[0][:share].T,
         summed[2].T,
         summed[3],
-        misc_sum[starts[2] : starts[3]].reshape(8, share),
-        misc_sum[starts[3] : starts[4]],
+        flat[: 8 * share].reshape(8, share),
+        flat[8 * share : 8 * share + share_inner],
     )
     squares = sum((jnp.sum(g * g) for g in grads))
     scalars = padded(jnp.stack([squares, loss_own, count_own]), 8, 128)

time: 586 us -> 558 us (0.952)
  matrix products: 139 us -> 75.5 us
  local copies, waits for them, and re-layouts: 40.9 us -> 60.7 us
  loops' own time: 0.53 us -> 8.74 us
  Pallas kernels: 314 us -> 321 us
    dot_general x11 -> x6, matrix products: 74.2 us -> 24.9 us  [contract(): lax.dot_general(left, right, (((left_dim,), (right_dim,)), ((), ())), pre...]
    another operation x1, loops' own time: 0.27 us -> 8.73 us  [on_device(): lax.while_loop(lambda state: state[0] < rounds, again, (jnp.int32(1), jnp...]
    transpose x1 -> x8, local copies, waits for them, and re-layouts: 0.28 us -> 7.47 us  [the longest x2 5.61 us: by_plane(): return blocks.transpose(1, 0, 2, 3, 4).reshape(planes, -1, lanes)]
    dot_general x6 -> x4, matrix products: 19.3 us -> 13.7 us  [the longest x1 4.69 us: on_device(): jnp.einsum('ptu,td->pud', active, grad_sum_low, preferred_element_type=f32)]
where the time goes in v2:
time: 558 us; the launch traced here: 550 us
  Pallas kernels  321 us (58%)
  matrix products  75.5 us (14%)
  other arithmetic  70 us (13%)
  local copies, waits for them, and re-layouts  60.7 us (11%)
  between operations  13.9 us (2%)
  loops' own time  8.74 us (2%)
    pallas_call x1, Pallas kernels, forward(): pl.pallas_call(functools.partial(forward_kernel, planes, ROOM), out_shape...  133 us
    pallas_call x1, Pallas kernels, give(): pl.pallas_call(functools.partial(give_kernel, planes, count), out_shape=[...  103 us
    dot_general x6, matrix products, contract(): lax.dot_general(left, right, (((left_dim,), (right_dim,)), ((), ())), pre...  24.9 us
    pallas_call x1, Pallas kernels, scatter_rows(): pl.pallas_call(functools.partial(scatter_kernel, planes, 1), out_shape=ja...  23.7 us
    pallas_call x1, Pallas kernels, rows(): pl.pallas_call(functools.partial(gather_kernel, planes, 1), out_shape=jax...  23.7 us
    pallas_call x2, Pallas kernels, small(): pl.pallas_call(functools.partial(small_kernel, planes), out_shape=jax.Sha...  23 us
    sub x8, other arithmetic, adamw(): return (weight - rate * (moved + decay * weight), first, second)  17.5 us
    pallas_call x1, Pallas kernels, ids(): pl.pallas_call(functools.partial(ids_kernel, planes), out_shape=[jax.Shap...  14.8 us

profile of v2, /device:TPU:0, one launch (start us, length us, event | category | flops | bytes accessed | tf_op | source)
XLA Modules:
  0.0 550.1 jit_solution(11982343153045737492)
XLA Ops:
  17.7 14.8 %ids.1 = (s32[8,24,128]{2,1,0:T(8,128)}, bf16[2,4,4,16,128]{4,3,2,1,0:T(8,128)(2,1)}) custom-call(s32[24,128]{1,0:T(8,128)} %pad_bitcast_fusion.x, bf16[16,128]{1,0:T(8,128)(2,1)} %fusion.77.small), custom_call_target="tpu_custom_call" | custom-call | tf_op jit(solution)/shard_map/ids/pallas_call | solution.py:797
  53.6 8.7 %while.24 = (s32[]{:T(128)}, f32[512,768]{1,0:T(8,128)S(1)}, s32[]{:T(128)}, s32[512]{0:T(512)S(1)}, s32[512]{0:T(512)S(1)}, /*index=5*/s32[16,1024]{1,0:T(8,128...) while((s32[]{:T(128)}, f32[512,768]{1,0:T(8,128)S(1)}, s32[]{:T(128)}, ...), condition=%wide.region_7.8_spmd, body=%wide.region_5.7_spmd.sunk | while | flops 3126939136 | bytes 9634425 | solution.py:1238
  62.4 133.3 %forward.1 = (bf16[4,4,2,48,768]{4,3,2,1,0:T(8,128)(2,1)}, bf16[4,4,2,96,576]{4,3,2,1,0:T(8,128)(2,1)}, bf16[4,4,2,96,768]{4,3,2,1,0:T(8,128)(2,1)}, bf16[4,4,2,...) custom-call(bf16[4,4,64,768]{3,2,1,0:T(8,128)(2,1)} %bitcast.253, ...), custom_call_target="tpu_custom_call" | custom-call | tf_op jit(solution)/shard_map/forward/pallas_call | solution.py:833
  202.4 4.5 copy.143
  206.9 3.2 fusion.110
  210.1 23.7 %rows.1 = bf16[4,4,2,64,768]{4,3,2,1,0:T(8,128)(2,1)} custom-call(bf16[64,768]{1,0:T(8,128)(2,1)} %get-tuple-element.261.refs_0_), custom_call_target="tpu_custom_call" | custom-call | tf_op jit(solution)/shard_map/rows/pallas_call | solution.py:885
  241.8 3.3 fusion.112
  245.1 3.2 copy-done.4
  251.6 12.7 %small.2 = f32[2,4,4,16,128]{4,3,2,1,0:T(8,128)} custom-call(f32[16,128]{1,0:T(8,128)} %add_bitcast_fusion.1.x), custom_call_target="tpu_custom_call" | custom-call | tf_op jit(solution)/shard_map/small/pallas_call | solution.py:898
  266.3 10.2 %fusion.94 = f32[960,768]{1,0:T(8,128)} fusion(bf16[2048,768]{1,0:T(8,128)(2,1)} %bitcast.248, f32[2048,960]{0,1:T(8,128)} %copy-done.4, s32[2048]{0:T(1024)S(1)} %copy-done.26, f32[2048]{0:T(1024)S(1)} %add_bitcast_fusion, f32[2048]{0:T(1024)S(1)} %copy-done.29), kind=kOutput, calls=%fused_computation.246 | convolution fusion | flops 3031695360 | bytes 13983744 | tf_op jit(solution)/shard_map/dot_general | solution.py:1005
  276.6 5.9 %convolution_convert_fusion = bf16[2048,768]{1,0:T(8,128)(2,1)} fusion(bf16[960,768]{1,0:T(8,128)(2,1)S(1)} %copy-done.19, f32[2048,960]{0,1:T(8,128)S(1)} %copy-done.5, s32[2048]{0:T(1024)S(1)} %copy-done.26, f32[2048]{0:T(1024)S(1)} %add_bitcast_fusion, f32[2048]{0:T(1024)S(1)} %copy-done.29), kind=kOutput, calls=%fused_computation.54 | convolution fusion | flops 3033268224 | bytes 12509184 | tf_op jit(solution)/shard_map/dot_general | solution.py:1291
  284.5 23.7 %scatter_rows.1 = f32[64,768]{1,0:T(8,128)} custom-call(bf16[4,4,2,64,768]{4,3,2,1,0:T(8,128)(2,1)} %bitcast.250), custom_call_target="tpu_custom_call" | custom-call | tf_op jit(solution)/shard_map/scatter_rows/pallas_call | solution.py:912
  311.2 4.7 convolution_convert_fusion.1
  325.5 3.3 convolution_convert_fusion.2
  343.0 3.7 fusion.30
  346.7 6.9 %multiply_reduce_fusion = (f32[12,512]{1,0:T(8,128)S(1)}, f32[12,512,512]{1,2,0:T(8,128)}) fusion(f32[12,512,512]{1,2,0:T(8,128)S(1)} %fusion.113, f32[12,512]{1,0:T(8,128)S(1)} %copy.144, pred[512,512]{0,1:T(8,128)(4,1)S(1)} %broadcast_compare_fusion, bf16[512,12,64]{0,2,1:T(8,128)(2,1)S(1)} %bitcast.245, f32[512,12,64]{0,2,1:T(8,128)S(1)} %bitcast.234, ...), kind=kOutput, calls=%fused_computation.27 | convolution fusion | flops 419162112 | bytes 27836464 | tf_op jit(solution)/shard_map/qhe,khe->hqk/dot_general | solution.py:1097
  353.6 7.3 %multiply_convert_fusion = bf16[12,512,512]{1,2,0:T(8,128)(2,1)S(1)} fusion(f32[12,512,512]{1,2,0:T(8,128)} %get-tuple-element.380, f32[12,512,512]{1,2,0:T(8,128)S(1)} %fusion.113, f32[12,512]{1,0:T(8,128)S(1)} %get-tuple-element.379, f32[12,512]{1,0:T(8,128)S(1)} %copy.144, pred[512,512]{0,1:T(8,128)(4,1)S(1)} %broadcast_compare_fusion), kind=kLoop, calls=%fused_computation.26 | loop fusion | flops 18874368 | bytes 31768576 | tf_op jit(solution)/shard_map/convert_element_type | solution.py:1099
  370.1 3.8 convert_bitcast_fusion
  374.5 5.9 %copy.155 = bf16[4,768,576]{2,1,0:T(8,128)(2,1)} copy(bf16[4,768,576]{1,2,0:T(8,128)(2,1)} %convert_bitcast_fusion) | data formatting | bytes 7077888 | tf_op jit(solution)/shard_map/convert_element_type | solution.py:1376
  384.9 3.6 fusion.23
  388.6 102.7 %give.1 = (bf16[4,4,64,768]{3,2,1,0:T(8,128)(2,1)}, f32[64,768]{1,0:T(8,128)}, f32[96,576]{1,0:T(8,128)}, f32[96,768]{1,0:T(8,128)}, f32[96,768]{1,0:T(8,128)}) custom-call(bf16[2,4,4,64,768]{4,3,2,1,0:T(8,128)(2,1)} %bitcast.246, bf16[4,4,2,64,768]{4,3,2,1,0:T(8,128)(2,1)} %maximum_maximum_fusion.refs_1_, bf16[4,4,2,96,576]{4,3,2,1,0:T(8,128)(2,1)} %bitcast.225, ...), custom_call_target="tpu_custom_call" | custom-call | tf_op jit(solution)/shard_map/give/pallas_call | solution.py:928
  501.8 4.4 fusion.29
  514.1 10.4 %small.3 = f32[2,4,4,8,128]{4,3,2,1,0:T(8,128)} custom-call(f32[8,128]{1,0:T(8,128)} %fusion.78.x), custom_call_target="tpu_custom_call" | custom-call | tf_op jit(solution)/shard_map/small/pallas_call | solution.py:898
  542.8 5.6 %multiply_subtract_fusion = (f32[960,768]{1,0:T(8,128)}, f32[960,768]{1,0:T(8,128)}, f32[960,768]{1,0:T(8,128)}) fusion(f32[960,768]{1,0:T(8,128)S(1)} %copy-done.3, f32[960,768]{1,0:T(8,128)S(1)} %get-tuple-element.278, f32[]{:T(128)S(6)} %div.211, f32[960,768]{1,0:T(8,128)S(1)} %copy-done.16, f32[960,768]{1,0:T(8,128)} %param.52), kind=kLoop, calls=%fused_computation.58 | loop fusion | flops 11796480 | bytes 20643844 | tf_op jit(solution)/shard_map/sub | solution.py:1113
  (267 shorter events, 126.8 us)
Async XLA Ops:
  8.5 32.4 %copy-start.25 = (s32[1,512]{1,0:T(1,128)}, s32[1,512]{1,0:T(1,128)S(1)}, u32[]{:S(2)}) copy-start(s32[1,512]{1,0:T(1,128)S(1)} %constant_dynamic-slice_fusion.refs_8_) | copy-start | bytes 6148
  32.5 9.4 %copy-start.24 = (bf16[2,4,4,16,128]{4,3,2,1,0:T(8,128)(2,1)S(1)}, bf16[2,4,4,16,128]{4,3,2,1,0:T(8,128)(2,1)}, u32[]{:S(2)}) copy-start(bf16[2,4,4,16,128]{4,3,2,1,0:T(8,128)(2,1)} %get-tuple-element.260) | copy-start | bytes 393220
  35.5 14.7 %copy-start.2 = (f32[960,768]{1,0:T(8,128)S(1)}, f32[960,768]{1,0:T(8,128)}, u32[]{:S(2)}) copy-start(f32[960,768]{1,0:T(8,128)} %param.36) | copy-start | bytes 8847364
  35.9 8.0 %copy-start.30 = (s32[512]{0:T(512)}, s32[512]{0:T(512)S(1)}, u32[]{:S(2)}) copy-start(s32[512]{0:T(512)S(1)} %get-tuple-element.362) | copy-start | bytes 6148
  42.7 7.6 %copy-start.34 = (s32[1024]{0:T(1024)S(1)}, s32[1024]{0:T(1024)}, u32[]{:S(2)}) copy-start(s32[1024]{0:T(1024)} %sub.230) | copy-start | bytes 12292
  202.4 31.4 %slice-start.6 = ((s8[4718592]{0:T(1024)(128)(4,1)}), s8[524288]{0:T(1024)(128)(4,1)S(1)}, s32[]{:S(2)}) async-start(s8[4718592]{0:T(1024)(128)(4,1)} %bitcast.238), calls=%async_computation.6 | async-start | bytes 1048576
  206.9 26.9 %slice-start.7 = ((s8[4718592]{0:T(1024)(128)(4,1)}), s8[4194304]{0:T(1024)(128)(4,1)S(1)}, s32[]{:S(2)}) async-start(s8[4718592]{0:T(1024)(128)(4,1)} %bitcast.238), calls=%async_computation.7 | async-start | bytes 8388608
  248.2 18.0 %copy-start.29 = (f32[2048]{0:T(1024)S(1)}, f32[2048]{0:T(1024)}, u32[]{:S(2)}) copy-start(f32[2048]{0:T(1024)} %convert_element_type.162) | copy-start | bytes 24580
  266.3 10.3 %copy-start.5 = (f32[2048,960]{0,1:T(8,128)S(1)}, f32[2048,960]{0,1:T(8,128)}, u32[]{:S(2)}) copy-start(f32[2048,960]{0,1:T(8,128)} %copy-done.4) | copy-start | bytes 23592964
  282.5 25.8 %copy-start.8 = (f32[512,768]{1,0:T(8,128)S(1)}, f32[512,768]{1,0:T(8,128)}, u32[]{:S(2)}) copy-start(f32[512,768]{1,0:T(8,128)} %get-tuple-element.265) | copy-start | bytes 4718596
  282.5 25.8 %copy-start.37 = (s32[64]{0:T(128)S(1)}, s32[64]{0:T(128)}, u32[]{:S(2)}) copy-start(s32[64]{0:T(128)} %get-tuple-element.370) | copy-start | bytes 772
  284.5 26.0 %copy-start.9 = (f32[512,768]{1,0:T(8,128)S(1)}, f32[512,768]{1,0:T(8,128)}, u32[]{:S(2)}) copy-start(f32[512,768]{1,0:T(8,128)} %get-tuple-element.265) | copy-start | bytes 4718596
  310.5 8.1 %slice-start = ((s8[4718592]{0:T(1024)(128)(4,1)}), s8[524288]{0:T(1024)(128)(4,1)S(1)}, s32[]{:S(2)}) async-start(s8[4718592]{0:T(1024)(128)(4,1)} %bitcast.216), calls=%async_computation | async-start | bytes 1048576
  370.1 10.3 %copy-start.13 = (bf16[512,768]{1,0:T(8,128)(2,1)}, bf16[512,768]{1,0:T(8,128)(2,1)S(1)}, u32[]{:S(2)}) copy-start(bf16[512,768]{1,0:T(8,128)(2,1)S(1)} %multiply_convert_fusion.2) | copy-start | bytes 2359300
  388.6 113.2 %copy-start.35 = (s32[1024]{0:T(1024)S(1)}, s32[1024]{0:T(1024)}, u32[]{:S(2)}) copy-start(s32[1024]{0:T(1024)} %sub.230) | copy-start | bytes 12292
  388.6 113.2 %copy-start.41 = (f32[960,768]{1,0:T(8,128)S(1)}, f32[960,768]{1,0:T(8,128)}, u32[]{:S(2)}) copy-start(f32[960,768]{1,0:T(8,128)} %fusion.94) | copy-start | bytes 8847364
  506.2 26.0 %copy-start.28 = (f32[8,24]{1,0:T(8,128)S(1)}, f32[8,24]{1,0:T(8,128)}, u32[]{:S(2)}) copy-start(f32[8,24]{1,0:T(8,128)} %param.42) | copy-start | bytes 2308
  506.2 25.9 %copy-start.32 = (f32[8,24]{1,0:T(8,128)S(1)}, f32[8,24]{1,0:T(8,128)}, u32[]{:S(2)}) copy-start(f32[8,24]{1,0:T(8,128)} %param.50) | copy-start | bytes 2308
  506.2 25.9 %copy-start.33 = (f32[8,24]{1,0:T(8,128)S(1)}, f32[8,24]{1,0:T(8,128)}, u32[]{:S(2)}) copy-start(f32[8,24]{1,0:T(8,128)} %param.58) | copy-start | bytes 2308
  506.2 32.4 %copy-start.20 = (f32[96,768]{1,0:T(8,128)S(1)}, f32[96,768]{1,0:T(8,128)}, u32[]{:S(2)}) copy-start(f32[96,768]{1,0:T(8,128)} %param.41) | copy-start | bytes 884740
  507.6 33.2 %copy-start.21 = (f32[768,96]{0,1:T(8,128)S(1)}, f32[768,96]{0,1:T(8,128)}, u32[]{:S(2)}) copy-start(f32[768,96]{0,1:T(8,128)} %param.40) | copy-start | bytes 884740
  532.2 8.7 %copy-start.22 = (f32[96,768]{1,0:T(8,128)S(1)}, f32[96,768]{1,0:T(8,128)}, u32[]{:S(2)}) copy-start(f32[96,768]{1,0:T(8,128)} %get-tuple-element.281) | copy-start | bytes 884740
  532.2 8.6 %copy-start.23 = (f32[768,96]{0,1:T(8,128)S(1)}, f32[768,96]{0,1:T(8,128)}, u32[]{:S(2)}) copy-start(f32[768,96]{0,1:T(8,128)} %param.48) | copy-start | bytes 884740
  534.4 8.5 %copy-start.16 = (f32[960,768]{1,0:T(8,128)S(1)}, f32[960,768]{1,0:T(8,128)}, u32[]{:S(2)}) copy-start(f32[960,768]{1,0:T(8,128)} %param.44) | copy-start | bytes 8847364
  (26 other events, 93.7 us)
